TPU v7x, 32 devices: a whole 2x2x4 slice. The times are simulated.
32 devices in a mesh: inner: 4 (over z), outer: 8 (over y, x, core).
Axes of the slice: x: 2, y: 2, z: 4, core: 2. Of those that a mesh axis runs over, the one named last changes fastest.
Arguments:
- features: bfloat16 [262144, 256], P(('inner', 'outer')), may hold values from -6 to 6
- tiles: bfloat16 [2048, 8, 128, 128], P(('inner', 'outer')), may hold values from -0.1875 to 0.1875
- tile_src: int32 [2048, 8], P(('inner', 'outer')), may hold values from 0 to 111, as said below
- tile_count: int32 [2048], P(('inner', 'outer')), may hold values from 1 to 8
- node_count: int32 [32], P(('inner', 'outer')), may hold values from 2730 to 8192
- boundary: int32 [32, 8], P(('inner', 'outer')), may hold values from 0 to 63, as said below
- send_inner: int32 [32, 4, 4], P(('inner', 'outer')), may hold values from 0 to 7
- count_inner: int32 [32, 4], P(('inner', 'outer')), may hold values from 0 to 4, as said below
- send_outer: int32 [32, 8, 4], P(('inner', 'outer')), may hold values from 0 to 7
- count_outer: int32 [32, 8], P(('inner', 'outer')), may hold values from 0 to 4, as said below
- w_first: bfloat16 [256, 256], replicated, may hold values from -0.375 to 0.375
- gamma: float32 [256], replicated, may hold values from 0.25 to 1.75
- beta: float32 [256], replicated, may hold values from -3 to 3
- w_second: bfloat16 [256, 256], replicated, may hold values from -0.375 to 0.375
- b_second: float32 [256], replicated, may hold values from -3 to 3
Outputs:
- updated: bfloat16 [262144, 256], P(('inner', 'outer'))
Inputs may be any that keep to these rules, and one draw needn't show every extreme that they name: `tile_src`: index into the partition's source table; a slot index that is read names a slot its sender fills. `boundary`: distinct block numbers within a partition. `count_inner`: zero toward the partition itself, at least one toward every other peer. `count_outer`: zero toward the partition itself, at least one toward every other peer.
All inputs are finite; a program needn't handle non-finite values.
Results may differ from a plain program's by a relative error of at most 0.0053.
Values may be sent and summed in bfloat16 or wider, within the bound.
A program may use at most 128 MiB of HBM per device.

v0:
```python
import math

import jax
import jax.numpy as jnp
from jax import lax
from jax.sharding import PartitionSpec as P

EPSILON = 1e-05


def packed(blocks, border, lists, counts, capacity):
    chosen = blocks[border[lists]]
    keep = jnp.arange(capacity)[None, :] < counts[:, None]
    return jnp.where(keep[:, :, None, None], chosen, jnp.zeros((), blocks.dtype))


def local(
    features,
    tiles,
    tile_src,
    tile_count,
    node_count,
    boundary,
    send_inner,
    count_inner,
    send_outer,
    count_outer,
    w_first,
    gamma,
    beta,
    w_second,
    b_second,
):
    node_dev, width = features.shape
    nblocks, per_block, block_rows = (tiles.shape[0], tiles.shape[1], tiles.shape[2])
    capacity = send_inner.shape[2]
    zero_bf = jnp.zeros((), jnp.bfloat16)
    filled = node_count[0]
    live = jnp.arange(node_dev) < filled
    features_live = jnp.where(live[:, None], features, zero_bf)
    blocks = features_live.reshape(nblocks, block_rows, width)
    border = boundary[0]
    from_inner = lax.all_to_all(
        packed(blocks, border, send_inner[0], count_inner[0], capacity),
        "inner",
        split_axis=0,
        concat_axis=0,
        tiled=True,
    )
    from_outer = lax.all_to_all(
        packed(blocks, border, send_outer[0], count_outer[0], capacity),
        "outer",
        split_axis=0,
        concat_axis=0,
        tiled=True,
    )
    table = jnp.concatenate(
        [
            blocks,
            from_inner.reshape(-1, block_rows, width),
            from_outer.reshape(-1, block_rows, width),
            jnp.zeros((1, block_rows, width), jnp.bfloat16),
        ],
        axis=0,
    )
    empty_slot = table.shape[0] - 1
    used = jnp.arange(per_block)[None, :] < tile_count[:, None]
    sources = jnp.where(used, tile_src, empty_slot)
    group = math.gcd(nblocks, 8)

    def aggregate(item):
        tile_group, source_group = item
        gathered = table[source_group]
        return jnp.einsum(
            "bjrk,bjkf->brf", tile_group, gathered, preferred_element_type=jnp.float32
        )

    summed = lax.map(
        aggregate,
        (
            tiles.reshape(-1, group, per_block, block_rows, block_rows),
            sources.reshape(-1, group, per_block),
        ),
    )
    combined = (features_live.astype(jnp.float32) + summed.reshape(node_dev, width)).astype(
        jnp.bfloat16
    )
    first = jnp.dot(combined, w_first, preferred_element_type=jnp.float32)
    count_local = filled.astype(jnp.float32).reshape(1)
    masked = jnp.where(live[:, None], first, 0.0)
    totals = lax.psum(
        (count_local, jnp.sum(masked, axis=0), jnp.sum(masked * masked, axis=0)), ("inner", "outer")
    )
    mean = totals[1] / totals[0]
    variance = totals[2] / totals[0] - mean * mean
    normed = jax.nn.relu(gamma * (first - mean) * lax.rsqrt(variance + EPSILON) + beta).astype(
        jnp.bfloat16
    )
    output = jnp.dot(normed, w_second, preferred_element_type=jnp.float32) + b_second
    return jnp.where(live[:, None], output, 0.0).astype(jnp.bfloat16)


def solution(mesh):
    in_specs = (
        P(("inner", "outer"), None),
        P(("inner", "outer"), None, None, None),
        P(("inner", "outer"), None),
        P(("inner", "outer")),
        P(("inner", "outer")),
        P(("inner", "outer"), None),
        P(("inner", "outer"), None, None),
        P(("inner", "outer"), None),
        P(("inner", "outer"), None, None),
        P(("inner", "outer"), None),
        P(),
        P(),
        P(),
        P(),
        P(),
    )
    out_specs = P(("inner", "outer"), None)
    return jax.shard_map(local, mesh=mesh, in_specs=in_specs, out_specs=out_specs, check_vma=False)
```

profile of v0, /device:TPU:0, one launch (start us, length us, event | category | flops | bytes accessed | tf_op | source)
XLA Modules:
  0.0 222.3 jit_solution(13318727625451619962)
XLA Ops:
  0.7 0.7 compare_select_fusion.4
  1.4 0.1 reshape.207
  1.5 1.3 gather_fusion.1
  2.8 0.1 gather.20
  2.9 0.1 reshape.215
  3.0 0.7 iota_compare_fusion.3
  3.7 5.2 %broadcast_select_fusion = bf16[8192,256]{1,0:T(8,128)(2,1)} fusion(bf16[8192,256]{1,0:T(8,128)(2,1)} %param.17, pred[8192]{0:T(1024)(128)(4,1)S(1)} %iota_compare_fusion), kind=kLoop, calls=%fused_computation.27 | loop fusion | flops 2097152 | bytes 8396800 | tf_op jit(solution)/shard_map/jit(_where)/select_n | solution.py:40
  9.0 2.8 %gather_fusion.2 = bf16[16,128,256]{2,1,0:T(8,128)(2,1)S(1)} fusion(bf16[64,128,256]{2,1,0:T(8,128)(2,1)} %bitcast.65, s32[1024]{0:T(1024)S(1)} %pad_clamp_fusion.3), kind=kCustom, calls=%fused_computation.2 | custom fusion | bytes 2097216 | tf_op jit(solution)/shard_map/gather | solution.py:12
  11.8 1.1 broadcast_select_fusion.2
  12.9 6.3 %all-to-all-start = ((bf16[4,4,128,256]{3,2,1,0:T(8,128)(2,1)}), bf16[4,4,128,256]{3,2,1,0:T(8,128)(2,1)S(1)}, u32[]{:S(2)}, u32[]{:S(2)}) async-start(bf16[4,4,128,256]{3,2,1,0:T(8,128)(2,1)} %broadcast_select_fusion.2), calls=%async_computation | async-start | bytes 2097152 | tf_op jit(solution)/shard_map/all_to_all | solution.py:43
  19.2 0.1 copy.23
  19.3 0.1 reshape.223
  19.4 0.7 gather_fusion.3
  20.2 0.1 copy.24
  20.3 0.1 copy.27
  20.5 2.9 %gather_fusion.4 = bf16[32,128,256]{2,1,0:T(8,128)(2,1)S(1)} fusion(bf16[64,128,256]{2,1,0:T(8,128)(2,1)} %bitcast.66, s32[1024]{0:T(1024)S(1)} %pad_clamp_fusion.1), kind=kCustom, calls=%fused_computation.4 | custom fusion | bytes 4194432 | tf_op jit(solution)/shard_map/gather | solution.py:12
  23.5 1.6 broadcast_select_fusion.1
  25.0 19.9 %all-to-all-done = bf16[4,4,128,256]{3,2,1,0:T(8,128)(2,1)S(1)} async-done(((bf16[4,4,128,256]{3,2,1,0:T(8,128)(2,1)}), bf16[4,4,128,256]{3,2,1,0:T(8,128)(2,1)S(1)}, u32[]{:S(2)}, u32[]{:S(2)}) %all-to-all-start) | async-done | bytes 1048608 | tf_op jit(solution)/shard_map/all_to_all | solution.py:43
  44.9 3.7 %all-to-all-start.1 = ((bf16[8,4,128,256]{3,2,1,0:T(8,128)(2,1)}), bf16[8,4,128,256]{3,2,1,0:T(8,128)(2,1)S(1)}, u32[]{:S(2)}, u32[]{:S(2)}) async-start(bf16[8,4,128,256]{3,2,1,0:T(8,128)(2,1)} %broadcast_select_fusion.1), calls=%async_computation.1 | async-start | bytes 4194304 | tf_op jit(solution)/shard_map/all_to_all | solution.py:50
  48.7 0.1 copy.22
  48.9 26.5 %all-to-all-done.1 = bf16[8,4,128,256]{3,2,1,0:T(8,128)(2,1)S(1)} async-done(((bf16[8,4,128,256]{3,2,1,0:T(8,128)(2,1)}), bf16[8,4,128,256]{3,2,1,0:T(8,128)(2,1)S(1)}, u32[]{:S(2)}, u32[]{:S(2)}) %all-to-all-start.1) | async-done | bytes 2097184 | tf_op jit(solution)/shard_map/all_to_all | solution.py:50
  75.3 6.0 %maximum_maximum_fusion = bf16[113,128,256]{2,1,0:T(8,128)(2,1)} fusion(bf16[32,128,256]{2,1,0:T(8,128)(2,1)S(1)} %bitcast.69, bf16[16,128,256]{2,1,0:T(8,128)(2,1)S(1)} %bitcast.71, bf16[64,128,256]{2,1,0:T(8,128)(2,1)} %bitcast.67, bf16[113]{0:T(256)(128)(2,1)S(1)} %pad.3.clone), kind=kLoop, calls=%fused_computation.21 | loop fusion | flops 11108352 | bytes 14745826 | tf_op jit(solution)/shard_map/concatenate | solution.py:57
  81.3 85.3 %while.10 = (s32[]{:T(128)}, f32[8,8,128,256]{3,2,1,0:T(8,128)}, bf16[8,8,8,128,128]{4,3,2,1,0:T(8,128)(2,1)}, s32[8,8,8]{2,1,0:T(8,128)S(1)}, bf16[113,128,256]{2,1,0:T(8,128)(2,1)}, /*index=5*/s32[]{:T(128)}) while((s32[]{:T(128)}, f32[8,8,128,256]{3,2,1,0:T(8,128)}, bf16[8,8,8,128,128]{4,3,2,1,0:T(8,128)(2,1)}, s32[8,8,8]{2,1,0:T(8,128)S(1)}, ...), condition=%wide.region_1.2_spmd, body=%wide.region_0.1_spmd.sunk | while | flops 536872128 | bytes 15735369 | solution.py:78
  81.4 0.1 reshape.251
  81.4 5.9 %gather_fusion = bf16[64,128,256]{2,1,0:T(8,128)(2,1)} fusion(bf16[113,128,256]{2,1,0:T(8,128)(2,1)} %get-tuple-element.98, s32[1024]{0:T(1024)S(1)} %pad_clamp_fusion.6), kind=kCustom, calls=%fused_computation.clone.1 | custom fusion | bytes 8388864 | tf_op jit(solution)/shard_map/while/body/eval_jaxpr/gather | solution.py:73
  87.4 4.6 %fusion.29 = f32[8,8,128,256]{3,2,1,0:T(8,128)} fusion(f32[8,8,128,256]{3,2,1,0:T(8,128)} %get-tuple-element.89, s32[]{:T(128)} %get-tuple-element.88, bf16[8,8,128,256]{3,2,1,0:T(8,128)(2,1)} %bitcast.64, bf16[8,8,8,128,128]{4,3,2,1,0:T(8,128)(2,1)} %get-tuple-element.96), kind=kOutput, calls=%fused_computation.9.clone.1 | convolution fusion | flops 536870912 | bytes 7341056 | tf_op jit(solution)/shard_map/while/body/eval_jaxpr/bjrk,bjkf->brf/dot_general | solution.py:74
  92.1 5.9 %gather_fusion = bf16[64,128,256]{2,1,0:T(8,128)(2,1)} fusion(bf16[113,128,256]{2,1,0:T(8,128)(2,1)} %get-tuple-element.98, s32[1024]{0:T(1024)S(1)} %pad_clamp_fusion.6), kind=kCustom, calls=%fused_computation.clone.1 | custom fusion | bytes 8388864 | tf_op jit(solution)/shard_map/while/body/eval_jaxpr/gather | solution.py:73
  98.0 4.7 %fusion.29 = f32[8,8,128,256]{3,2,1,0:T(8,128)} fusion(f32[8,8,128,256]{3,2,1,0:T(8,128)} %get-tuple-element.89, s32[]{:T(128)} %get-tuple-element.88, bf16[8,8,128,256]{3,2,1,0:T(8,128)(2,1)} %bitcast.64, bf16[8,8,8,128,128]{4,3,2,1,0:T(8,128)(2,1)} %get-tuple-element.96), kind=kOutput, calls=%fused_computation.9.clone.1 | convolution fusion | flops 536870912 | bytes 7341056 | tf_op jit(solution)/shard_map/while/body/eval_jaxpr/bjrk,bjkf->brf/dot_general | solution.py:74
  102.7 0.1 reshape.251
  102.8 5.9 %gather_fusion = bf16[64,128,256]{2,1,0:T(8,128)(2,1)} fusion(bf16[113,128,256]{2,1,0:T(8,128)(2,1)} %get-tuple-element.98, s32[1024]{0:T(1024)S(1)} %pad_clamp_fusion.6), kind=kCustom, calls=%fused_computation.clone.1 | custom fusion | bytes 8388864 | tf_op jit(solution)/shard_map/while/body/eval_jaxpr/gather | solution.py:73
  108.7 4.6 %fusion.29 = f32[8,8,128,256]{3,2,1,0:T(8,128)} fusion(f32[8,8,128,256]{3,2,1,0:T(8,128)} %get-tuple-element.89, s32[]{:T(128)} %get-tuple-element.88, bf16[8,8,128,256]{3,2,1,0:T(8,128)(2,1)} %bitcast.64, bf16[8,8,8,128,128]{4,3,2,1,0:T(8,128)(2,1)} %get-tuple-element.96), kind=kOutput, calls=%fused_computation.9.clone.1 | convolution fusion | flops 536870912 | bytes 7341056 | tf_op jit(solution)/shard_map/while/body/eval_jaxpr/bjrk,bjkf->brf/dot_general | solution.py:74
  113.3 0.1 reshape.251
  113.4 5.9 %gather_fusion = bf16[64,128,256]{2,1,0:T(8,128)(2,1)} fusion(bf16[113,128,256]{2,1,0:T(8,128)(2,1)} %get-tuple-element.98, s32[1024]{0:T(1024)S(1)} %pad_clamp_fusion.6), kind=kCustom, calls=%fused_computation.clone.1 | custom fusion | bytes 8388864 | tf_op jit(solution)/shard_map/while/body/eval_jaxpr/gather | solution.py:73
  119.4 4.6 %fusion.29 = f32[8,8,128,256]{3,2,1,0:T(8,128)} fusion(f32[8,8,128,256]{3,2,1,0:T(8,128)} %get-tuple-element.89, s32[]{:T(128)} %get-tuple-element.88, bf16[8,8,128,256]{3,2,1,0:T(8,128)(2,1)} %bitcast.64, bf16[8,8,8,128,128]{4,3,2,1,0:T(8,128)(2,1)} %get-tuple-element.96), kind=kOutput, calls=%fused_computation.9.clone.1 | convolution fusion | flops 536870912 | bytes 7341056 | tf_op jit(solution)/shard_map/while/body/eval_jaxpr/bjrk,bjkf->brf/dot_general | solution.py:74
  124.0 0.1 reshape.251
  124.1 5.9 %gather_fusion = bf16[64,128,256]{2,1,0:T(8,128)(2,1)} fusion(bf16[113,128,256]{2,1,0:T(8,128)(2,1)} %get-tuple-element.98, s32[1024]{0:T(1024)S(1)} %pad_clamp_fusion.6), kind=kCustom, calls=%fused_computation.clone.1 | custom fusion | bytes 8388864 | tf_op jit(solution)/shard_map/while/body/eval_jaxpr/gather | solution.py:73
  130.0 4.6 %fusion.29 = f32[8,8,128,256]{3,2,1,0:T(8,128)} fusion(f32[8,8,128,256]{3,2,1,0:T(8,128)} %get-tuple-element.89, s32[]{:T(128)} %get-tuple-element.88, bf16[8,8,128,256]{3,2,1,0:T(8,128)(2,1)} %bitcast.64, bf16[8,8,8,128,128]{4,3,2,1,0:T(8,128)(2,1)} %get-tuple-element.96), kind=kOutput, calls=%fused_computation.9.clone.1 | convolution fusion | flops 536870912 | bytes 7341056 | tf_op jit(solution)/shard_map/while/body/eval_jaxpr/bjrk,bjkf->brf/dot_general | solution.py:74
  134.7 5.9 %gather_fusion = bf16[64,128,256]{2,1,0:T(8,128)(2,1)} fusion(bf16[113,128,256]{2,1,0:T(8,128)(2,1)} %get-tuple-element.98, s32[1024]{0:T(1024)S(1)} %pad_clamp_fusion.6), kind=kCustom, calls=%fused_computation.clone.1 | custom fusion | bytes 8388864 | tf_op jit(solution)/shard_map/while/body/eval_jaxpr/gather | solution.py:73
  140.7 4.6 %fusion.29 = f32[8,8,128,256]{3,2,1,0:T(8,128)} fusion(f32[8,8,128,256]{3,2,1,0:T(8,128)} %get-tuple-element.89, s32[]{:T(128)} %get-tuple-element.88, bf16[8,8,128,256]{3,2,1,0:T(8,128)(2,1)} %bitcast.64, bf16[8,8,8,128,128]{4,3,2,1,0:T(8,128)(2,1)} %get-tuple-element.96), kind=kOutput, calls=%fused_computation.9.clone.1 | convolution fusion | flops 536870912 | bytes 7341056 | tf_op jit(solution)/shard_map/while/body/eval_jaxpr/bjrk,bjkf->brf/dot_general | solution.py:74
  145.4 5.9 %gather_fusion = bf16[64,128,256]{2,1,0:T(8,128)(2,1)} fusion(bf16[113,128,256]{2,1,0:T(8,128)(2,1)} %get-tuple-element.98, s32[1024]{0:T(1024)S(1)} %pad_clamp_fusion.6), kind=kCustom, calls=%fused_computation.clone.1 | custom fusion | bytes 8388864 | tf_op jit(solution)/shard_map/while/body/eval_jaxpr/gather | solution.py:73
  151.3 4.6 %fusion.29 = f32[8,8,128,256]{3,2,1,0:T(8,128)} fusion(f32[8,8,128,256]{3,2,1,0:T(8,128)} %get-tuple-element.89, s32[]{:T(128)} %get-tuple-element.88, bf16[8,8,128,256]{3,2,1,0:T(8,128)(2,1)} %bitcast.64, bf16[8,8,8,128,128]{4,3,2,1,0:T(8,128)(2,1)} %get-tuple-element.96), kind=kOutput, calls=%fused_computation.9.clone.1 | convolution fusion | flops 536870912 | bytes 7341056 | tf_op jit(solution)/shard_map/while/body/eval_jaxpr/bjrk,bjkf->brf/dot_general | solution.py:74
  156.1 5.9 %gather_fusion = bf16[64,128,256]{2,1,0:T(8,128)(2,1)} fusion(bf16[113,128,256]{2,1,0:T(8,128)(2,1)} %get-tuple-element.98, s32[1024]{0:T(1024)S(1)} %pad_clamp_fusion.6), kind=kCustom, calls=%fused_computation.clone.1 | custom fusion | bytes 8388864 | tf_op jit(solution)/shard_map/while/body/eval_jaxpr/gather | solution.py:73
  162.0 4.7 %fusion.29 = f32[8,8,128,256]{3,2,1,0:T(8,128)} fusion(f32[8,8,128,256]{3,2,1,0:T(8,128)} %get-tuple-element.89, s32[]{:T(128)} %get-tuple-element.88, bf16[8,8,128,256]{3,2,1,0:T(8,128)(2,1)} %bitcast.64, bf16[8,8,8,128,128]{4,3,2,1,0:T(8,128)(2,1)} %get-tuple-element.96), kind=kOutput, calls=%fused_computation.9.clone.1 | convolution fusion | flops 536870912 | bytes 7341056 | tf_op jit(solution)/shard_map/while/body/eval_jaxpr/bjrk,bjkf->brf/dot_general | solution.py:74
  166.6 5.5 %fusion.12 = bf16[8192,256]{1,0:T(8,128)(2,1)S(1)} fusion(f32[8,8,128,256]{3,2,1,0:T(8,128)} %get-tuple-element.32, bf16[8192,256]{1,0:T(8,128)(2,1)} %param.17, pred[8192]{0:T(1024)(128)(4,1)S(1)} %iota_compare_fusion), kind=kLoop, calls=%fused_computation.17 | loop fusion | flops 8388608 | bytes 16785408 | tf_op jit(solution)/shard_map/convert_element_type | solution.py:85
  172.3 6.5 %multiply_reduce_fusion = (f32[256]{0:T(256)S(1)}, f32[256]{0:T(256)S(1)}, f32[8192,256]{1,0:T(8,128)}) fusion(pred[8192]{0:T(1024)(128)(4,1)S(1)} %iota_compare_fusion, bf16[8192,256]{1,0:T(8,128)(2,1)S(1)} %fusion.12, bf16[256,256]{1,0:T(8,128)(2,1)S(1)} %copy-done), kind=kOutput, calls=%fused_computation.19 | convolution fusion | flops 1082129920 | bytes 12724224 | tf_op jit(solution)/shard_map/dot_general | solution.py:88
  178.7 36.8 %all-reduce = (f32[256]{0:T(256)S(1)}, f32[]{:T(128)}, f32[256]{0:T(256)S(1)}) all-reduce(f32[256]{0:T(256)S(1)} %get-tuple-element.34, f32[]{:T(128)S(6)} %convert_element_type.17, f32[256]{0:T(256)S(1)} %get-tuple-element.33), channel_id=1, replica_groups=mesh['inner'=4,'outer'=8] {'inner','outer'}, use_global_device_ids=true, to_apply=%region_3.4 | all-reduce | flops 513 | bytes 4104 | tf_op jit(solution)/shard_map/psum | solution.py:91
  215.6 0.7 add_rsqrt_fusion
  216.3 6.1 %fusion.11 = bf16[8192,256]{1,0:T(8,128)(2,1)} fusion(bf16[256,256]{1,0:T(8,128)(2,1)S(1)} %copy-done.5, f32[8192,256]{1,0:T(8,128)} %get-tuple-element.50, f32[256]{0:T(256)S(1)} %copy-done.6, f32[256]{0:T(256)S(1)} %copy-done.7, f32[256]{0:T(256)S(1)} %get-tuple-element.48, f32[256]{0:T(256)S(1)} %get-tuple-element.49, f32[256]{0:T(256)S(1)} %copy-done.8, ...), kind=kOutput, calls=%fused_computation.15 | convolution fusion | flops 1092616192 | bytes 12727296 | tf_op jit(solution)/shard_map/dot_general | solution.py:99
  (54 shorter events, 0.9 us)
Async XLA Ops:
  0.0 172.2 %copy-start = (bf16[256,256]{1,0:T(8,128)(2,1)S(1)}, bf16[256,256]{1,0:T(8,128)(2,1)}, u32[]{:S(2)}) copy-start(bf16[256,256]{1,0:T(8,128)(2,1)} %param.27) | copy-start | bytes 393220
  2.8 16.4 %copy-start.3 = (s32[1,8,4]{1,2,0:T(4,128)S(1)}, s32[1,8,4]{1,2,0:T(4,128)}, u32[]{:S(2)}) copy-start(s32[1,8,4]{1,2,0:T(4,128)} %param.25) | copy-start | bytes 388
  2.8 16.6 %copy-start.1 = (s32[1,8]{1,0:T(1,128)S(1)}, s32[1,8]{1,0:T(1,128)}, u32[]{:S(2)}) copy-start(s32[1,8]{1,0:T(1,128)} %param.22) | copy-start | bytes 100
  9.0 14.4 %copy-start.9 = (s32[1,8]{1,0:T(1,128)S(1)}, s32[1,8]{1,0:T(1,128)}, u32[]{:S(2)}) copy-start(s32[1,8]{1,0:T(1,128)} %param.26) | copy-start | bytes 100
  12.9 32.0 %all-to-all-start = ((bf16[4,4,128,256]{3,2,1,0:T(8,128)(2,1)}), bf16[4,4,128,256]{3,2,1,0:T(8,128)(2,1)S(1)}, u32[]{:S(2)}, u32[]{:S(2)}) async-start(bf16[4,4,128,256]{3,2,1,0:T(8,128)(2,1)} %broadcast_select_fusion.2), calls=%async_computation | async-start | bytes 2097152 | tf_op jit(solution)/shard_map/all_to_all | solution.py:43
  19.4 29.3 %copy-start.2 = (s32[64,8]{0,1:T(8,128)S(1)}, s32[64,8]{0,1:T(8,128)}, u32[]{:S(2)}) copy-start(s32[64,8]{0,1:T(8,128)} %param.19) | copy-start | bytes 6148
  19.4 29.3 %copy-start.4 = (s32[64]{0:T(128)S(1)}, s32[64]{0:T(128)}, u32[]{:S(2)}) copy-start(s32[64]{0:T(128)} %param.20) | copy-start | bytes 772
  44.9 30.4 %all-to-all-start.1 = ((bf16[8,4,128,256]{3,2,1,0:T(8,128)(2,1)}), bf16[8,4,128,256]{3,2,1,0:T(8,128)(2,1)S(1)}, u32[]{:S(2)}, u32[]{:S(2)}) async-start(bf16[8,4,128,256]{3,2,1,0:T(8,128)(2,1)} %broadcast_select_fusion.1), calls=%async_computation.1 | async-start | bytes 4194304 | tf_op jit(solution)/shard_map/all_to_all | solution.py:50
  172.2 44.0 %copy-start.5 = (bf16[256,256]{1,0:T(8,128)(2,1)S(1)}, bf16[256,256]{1,0:T(8,128)(2,1)}, u32[]{:S(2)}) copy-start(bf16[256,256]{1,0:T(8,128)(2,1)} %param.30) | copy-start | bytes 393220
  172.2 44.0 %copy-start.6 = (f32[256]{0:T(256)S(1)}, f32[256]{0:T(256)}, u32[]{:S(2)}) copy-start(f32[256]{0:T(256)} %param.31) | copy-start | bytes 3076
  172.2 44.0 %copy-start.7 = (f32[256]{0:T(256)S(1)}, f32[256]{0:T(256)}, u32[]{:S(2)}) copy-start(f32[256]{0:T(256)} %param.29) | copy-start | bytes 3076
  172.2 44.0 %copy-start.8 = (f32[256]{0:T(256)S(1)}, f32[256]{0:T(256)}, u32[]{:S(2)}) copy-start(f32[256]{0:T(256)} %param.28) | copy-start | bytes 3076
where the time goes:
time: 224 us; the launch traced here: 222 us
  local copies, waits for them, and re-layouts  56.8 us (25%)
  matrix products  49.6 us (22%)
  waiting for transfers between devices  46.4 us (21%)
  blocking collectives  36.8 us (16%)
  other arithmetic  21.8 us (10%)
  starting transfers between devices  10 us (4%)
    gather x8, local copies, waits for them, and re-layouts, aggregate(): gathered = table[source_group]  47.4 us
    dot_general x8, matrix products, aggregate(): jnp.einsum('bjrk,bjkf->brf', tile_group, gathered, preferred_element_type...  37.1 us
    psum x1, blocking collectives, local(): lax.psum((count_local, jnp.sum(masked, axis=0), jnp.sum(masked * masked,...  36.8 us
    all_to_all x1, waiting for transfers between devices, local(): lax.all_to_all(packed(blocks, border, send_outer[0], count_outer[0], capa...  26.5 us
    all_to_all x1, waiting for transfers between devices, local(): lax.all_to_all(packed(blocks, border, send_inner[0], count_inner[0], capa...  19.9 us
    gather x7, local copies, waits for them, and re-layouts, packed(): chosen = blocks[border[lists]]  7.94 us
    dot_general x1, matrix products, local(): first = jnp.dot(combined, w_first, preferred_element_type=jnp.float32)  6.45 us
    all_to_all x1, starting transfers between devices, local(): lax.all_to_all(packed(blocks, border, send_inner[0], count_inner[0], capa...  6.32 us
  transfers between devices with their start and end apart: 2, of which 2 were waited for; matrix products, arithmetic and copies ran while one was open for 3% of the time, Pallas kernels for 0%

commit v1 on v0

v1 whole, which is shorter than its diff:
```python
import functools

import jax
import jax.numpy as jnp
from jax import lax
from jax.experimental import pallas as pl
from jax.experimental.pallas import tpu as pltpu
from jax.sharding import PartitionSpec as P

EPSILON = 1e-05
MESH = pl.DeviceIdType.MESH
BF16 = jnp.bfloat16
F32 = jnp.float32
DEPTH = 4
GROUP = 4


def peers_of(n_inner, n_outer):
    i, o = lax.axis_index("inner"), lax.axis_index("outer")
    inner = [((lax.rem(i + k, n_inner), o), k) for k in range(1, n_inner)]
    outer = [((i, lax.rem(o + k, n_outer)), k) for k in range(1, n_outer)]
    return inner, outer


def enter(partners):
    barrier = pltpu.get_barrier_semaphore()
    for device, _ in partners:
        pl.semaphore_signal(barrier, inc=1, device_id=device, device_id_type=MESH)
    pl.semaphore_wait(barrier, len(partners))


def exchange_kernel(
    n_inner,
    n_outer,
    src_ref,
    count_ref,
    node_ref,
    border_ref,
    send_in_ref,
    send_out_ref,
    feat_ref,
    tile_ref,
    recv_ref,
    part_ref,
    table,
    packed,
    tile_buf,
    part_buf,
    feat_sem,
    zero_sem,
    tile_sem,
    part_sem,
    send_sem,
    recv_sem,
):
    nb, per_block, rows = tile_ref.shape[0], tile_ref.shape[1], tile_ref.shape[2]
    width = feat_ref.shape[2]
    cap = send_in_ref.shape[2]
    i, o = lax.axis_index("inner"), lax.axis_index("outer")
    inner, outer = peers_of(n_inner, n_outer)
    filled = node_ref[0]
    row_ids = lax.broadcasted_iota(jnp.int32, (rows, width), 0)

    feats = pltpu.make_async_copy(feat_ref, table.at[pl.ds(0, nb)], feat_sem)
    feats.start()

    def tile_copy(b, slot):
        return pltpu.make_async_copy(tile_ref.at[b], tile_buf.at[slot], tile_sem.at[slot])

    def part_copy(b, slot):
        return pltpu.make_async_copy(part_buf.at[slot], part_ref.at[b], part_sem.at[slot])

    for d in range(DEPTH):
        tile_copy(d, d).start()
    enter(inner + outer)
    feats.wait()
    table[nb] = jnp.zeros((rows, width), BF16)

    def live_block(block):
        data = table[block].astype(F32)
        return jnp.where(row_ids < filled - block * rows, data, 0.0).astype(BF16)

    copies = []
    order = []
    for k in range(max(n_inner, n_outer)):
        if k < len(inner):
            order.append((inner[k], True))
        if k < len(outer):
            order.append((outer[k], False))
    for at, ((device, step), is_inner) in enumerate(order):
        for c in range(cap):
            if is_inner:
                entry = send_in_ref[0, device[0], c]
            else:
                entry = send_out_ref[0, device[1], c]
            packed[at, c] = live_block(border_ref[0, entry])
        first_slot = i * cap if is_inner else (n_inner + o) * cap
        copy = pltpu.make_async_remote_copy(
            src_ref=packed.at[at],
            dst_ref=recv_ref.at[pl.ds(first_slot, cap)],
            send_sem=send_sem.at[at],
            recv_sem=recv_sem.at[at],
            device_id=device,
            device_id_type=MESH,
        )
        copy.start()
        copies.append(copy)

    @pl.loop(0, nb)
    def _(block):
        table[block] = live_block(block)

    last = recv_ref.shape[0] - 1
    zeros = pltpu.make_async_copy(table.at[nb], recv_ref.at[last], zero_sem)
    zeros.start()

    def one(b, slot, wait_part, more):
        tile_copy(b, slot).wait()
        used = count_ref[b]
        total = table[b].astype(F32)
        for pair in range(per_block // 2):
            weights, sources = [], []
            for j in (2 * pair, 2 * pair + 1):
                s = src_ref[b, j]
                ok = jnp.logical_and(s < nb, j < used)
                sources.append(table[jnp.where(ok, s, nb)])
                weights.append(tile_buf[slot, j])
            total += jnp.dot(
                jnp.concatenate(weights, axis=1),
                jnp.concatenate(sources, axis=0),
                preferred_element_type=F32,
            )
        if wait_part:
            part_copy(b - DEPTH, slot).wait()
        part_buf[slot] = total
        part_copy(b, slot).start()
        if more:
            tile_copy(b + DEPTH, slot).start()

    for d in range(DEPTH):
        one(d, d, False, True)

    @pl.loop(1, nb // DEPTH - 1)
    def _(g):
        for d in range(DEPTH):
            one(g * DEPTH + d, d, True, True)

    for d in range(DEPTH):
        one(nb - DEPTH + d, d, True, False)
    for d in range(DEPTH):
        part_copy(nb - DEPTH + d, d).wait()
    zeros.wait()
    for copy in copies:
        copy.wait()


def exchange(mesh_sizes, tile_src, tile_count, node_count, boundary, send_inner, send_outer, blocks, tiles):
    n_inner, n_outer = mesh_sizes
    nb, per_block, rows = tiles.shape[:3]
    width = blocks.shape[2]
    cap = send_inner.shape[2]
    slots = (n_inner + n_outer) * cap + 1
    partners = n_inner + n_outer - 2
    smem = pl.BlockSpec(memory_space=pltpu.SMEM)
    hbm = pl.BlockSpec(memory_space=pl.ANY)
    return pl.pallas_call(
        functools.partial(exchange_kernel, n_inner, n_outer),
        out_shape=(
            jax.ShapeDtypeStruct((slots, rows, width), BF16),
            jax.ShapeDtypeStruct((nb, rows, width), F32),
        ),
        in_specs=[smem] * 6 + [hbm] * 2,
        out_specs=(hbm, hbm),
        scratch_shapes=[
            pltpu.VMEM((nb + 1, rows, width), BF16),
            pltpu.VMEM((partners, cap, rows, width), BF16),
            pltpu.VMEM((DEPTH, per_block, rows, rows), BF16),
            pltpu.VMEM((DEPTH, rows, width), F32),
            pltpu.SemaphoreType.DMA,
            pltpu.SemaphoreType.DMA,
            pltpu.SemaphoreType.DMA((DEPTH,)),
            pltpu.SemaphoreType.DMA((DEPTH,)),
            pltpu.SemaphoreType.DMA((partners,)),
            pltpu.SemaphoreType.DMA((partners,)),
        ],
        compiler_params=pltpu.CompilerParams(
            collective_id=0, has_side_effects=True, vmem_limit_bytes=40 << 20
        ),
    )(tile_src, tile_count, node_count, boundary, send_inner, send_outer, blocks, tiles)


def remote_kernel(
    src_ref, count_ref, node_ref, recv_ref, tile_ref, part_ref, w_ref, out_ref, stats_ref
):
    step = pl.program_id(0)
    nb_all = src_ref.shape[0]
    group, per_block, rows = tile_ref.shape[:3]
    width = part_ref.shape[2]
    zero_slot = recv_ref.shape[0] - 1
    filled = node_ref[0]

    @pl.when(step == 0)
    def _():
        stats_ref[...] = jnp.zeros_like(stats_ref)

    found = []
    for g in range(group):
        b = step * group + g
        used = count_ref[b]
        code, n = jnp.int32(0), jnp.int32(0)
        for j in range(per_block):
            hit = jnp.logical_and(src_ref[b, j] >= nb_all, j < used).astype(jnp.int32)
            code = code + hit * jnp.left_shift(jnp.int32(j), 3 * n)
            n = n + hit
        found.append((b, code, n))

    def pair_product(g, pair):
        b, code, n = found[g]
        weights, sources = [], []
        for rank in (2 * pair, 2 * pair + 1):
            j = jnp.bitwise_and(jnp.right_shift(code, 3 * rank), 7)
            slot = jnp.where(rank < n, src_ref[b, j] - nb_all, zero_slot)
            sources.append(recv_ref[slot])
            weights.append(tile_ref[g, j])
        return jnp.dot(
            jnp.concatenate(weights, axis=1),
            jnp.concatenate(sources, axis=0),
            preferred_element_type=F32,
        )

    for g in range(group):
        part_ref[g] += pair_product(g, 0)
    for g in range(group):
        for pair in range(1, per_block // 2):

            @pl.when(found[g][2] > 2 * pair)
            def _():
                part_ref[g] += pair_product(g, pair)

    combined = part_ref[...].reshape(group * rows, width).astype(BF16)
    out_ref[...] = combined
    first = jnp.dot(combined, w_ref[...], preferred_element_type=F32)
    row_ids = lax.broadcasted_iota(jnp.int32, first.shape, 0)
    kept = jnp.where(row_ids < filled - step * group * rows, first, 0.0)
    stats_ref[0:1, :] += jnp.sum(kept, axis=0, keepdims=True)
    stats_ref[1:2, :] += jnp.sum(kept * kept, axis=0, keepdims=True)

    @pl.when(step == 0)
    def _():
        stats_ref[2:3, :] = jnp.full((1, stats_ref.shape[1]), filled.astype(F32))


def remote_tiles(tile_src, tile_count, node_count, recv, tiles, part, w_first):
    nb, per_block, rows = tiles.shape[:3]
    width = part.shape[2]
    hidden = w_first.shape[1]
    return pl.pallas_call(
        remote_kernel,
        grid_spec=pltpu.PrefetchScalarGridSpec(
            num_scalar_prefetch=3,
            grid=(nb // GROUP,),
            in_specs=[
                pl.BlockSpec(recv.shape, lambda s, *_: (0, 0, 0)),
                pl.BlockSpec((GROUP, per_block, rows, rows), lambda s, *_: (s, 0, 0, 0)),
                pl.BlockSpec((GROUP, rows, width), lambda s, *_: (s, 0, 0)),
                pl.BlockSpec(w_first.shape, lambda s, *_: (0, 0)),
            ],
            out_specs=[
                pl.BlockSpec((GROUP * rows, width), lambda s, *_: (s, 0)),
                pl.BlockSpec((8, hidden), lambda s, *_: (0, 0)),
            ],
        ),
        out_shape=(
            jax.ShapeDtypeStruct((nb * rows, width), BF16),
            jax.ShapeDtypeStruct((8, hidden), F32),
        ),
        compiler_params=pltpu.CompilerParams(vmem_limit_bytes=40 << 20),
    )(tile_src, tile_count, node_count, recv, tiles, part, w_first)


def totals_kernel(n_inner, n_outer, stats_ref, out_ref, first_buf, second_buf, mid, send_sem, recv_sem):
    i, o = lax.axis_index("inner"), lax.axis_index("outer")
    inner, outer = peers_of(n_inner, n_outer)
    enter(inner + outer)

    def round_of(partners, source, buf, me, base):
        copies = []
        for at, (device, _) in enumerate(partners):
            copy = pltpu.make_async_remote_copy(
                src_ref=source,
                dst_ref=buf.at[me],
                send_sem=send_sem.at[base + at],
                recv_sem=recv_sem.at[base + at],
                device_id=device,
                device_id_type=MESH,
            )
            copy.start()
            copies.append(copy)
        buf[me] = source[...]
        for copy in copies:
            copy.wait()
        return jnp.sum(buf[...], axis=0)

    mid[...] = round_of(outer, stats_ref, first_buf, o, 0)
    out_ref[...] = round_of(inner, mid, second_buf, i, len(outer))


def all_totals(mesh_sizes, stats):
    n_inner, n_outer = mesh_sizes
    partners = n_inner + n_outer - 2
    vmem = pl.BlockSpec(memory_space=pltpu.VMEM)
    return pl.pallas_call(
        functools.partial(totals_kernel, n_inner, n_outer),
        out_shape=jax.ShapeDtypeStruct(stats.shape, F32),
        in_specs=[vmem],
        out_specs=vmem,
        scratch_shapes=[
            pltpu.VMEM((n_outer,) + stats.shape, F32),
            pltpu.VMEM((n_inner,) + stats.shape, F32),
            pltpu.VMEM(stats.shape, F32),
            pltpu.SemaphoreType.DMA((partners,)),
            pltpu.SemaphoreType.DMA((partners,)),
        ],
        compiler_params=pltpu.CompilerParams(collective_id=1, has_side_effects=True),
    )(stats)


def finish_kernel(
    node_ref, totals_ref, combined_ref, w1_ref, gamma_ref, beta_ref, w2_ref, bias_ref, out_ref
):
    rows = out_ref.shape[0]
    filled = node_ref[0]
    count = totals_ref[2:3, :]
    mean = totals_ref[0:1, :] / count
    variance = totals_ref[1:2, :] / count - mean * mean
    scale = gamma_ref[...] * lax.rsqrt(variance + EPSILON)
    first = jnp.dot(combined_ref[...], w1_ref[...], preferred_element_type=F32)
    normed = jnp.maximum(scale * (first - mean) + beta_ref[...], 0.0).astype(BF16)
    output = jnp.dot(normed, w2_ref[...], preferred_element_type=F32) + bias_ref[...]
    row_ids = lax.broadcasted_iota(jnp.int32, output.shape, 0)
    live = row_ids < filled - pl.program_id(0) * rows
    out_ref[...] = jnp.where(live, output, 0.0).astype(BF16)


def finish(node_count, totals, combined, w_first, gamma, beta, w_second, b_second):
    nodes, width = combined.shape
    hidden = w_first.shape[1]
    rows = nodes // 8
    whole = lambda s, *_: (0, 0)
    return pl.pallas_call(
        finish_kernel,
        grid_spec=pltpu.PrefetchScalarGridSpec(
            num_scalar_prefetch=1,
            grid=(nodes // rows,),
            in_specs=[
                pl.BlockSpec(totals.shape, whole),
                pl.BlockSpec((rows, width), lambda s, *_: (s, 0)),
                pl.BlockSpec(w_first.shape, whole),
                pl.BlockSpec((1, hidden), whole),
                pl.BlockSpec((1, hidden), whole),
                pl.BlockSpec(w_second.shape, whole),
                pl.BlockSpec((1, width), whole),
            ],
            out_specs=pl.BlockSpec((rows, width), lambda s, *_: (s, 0)),
        ),
        out_shape=jax.ShapeDtypeStruct((nodes, width), BF16),
        compiler_params=pltpu.CompilerParams(vmem_limit_bytes=40 << 20),
    )(
        node_count,
        totals,
        combined,
        w_first,
        gamma.reshape(1, -1),
        beta.reshape(1, -1),
        w_second,
        b_second.reshape(1, -1),
    )


def local(
    mesh_sizes,
    features,
    tiles,
    tile_src,
    tile_count,
    node_count,
    boundary,
    send_inner,
    count_inner,
    send_outer,
    count_outer,
    w_first,
    gamma,
    beta,
    w_second,
    b_second,
):
    nblocks, _, rows = tiles.shape[:3]
    blocks = features.reshape(nblocks, rows, features.shape[1])
    recv, part = exchange(
        mesh_sizes, tile_src, tile_count, node_count, boundary, send_inner, send_outer, blocks, tiles
    )
    combined, stats = remote_tiles(tile_src, tile_count, node_count, recv, tiles, part, w_first)
    totals = all_totals(mesh_sizes, stats)
    return finish(node_count, totals, combined, w_first, gamma, beta, w_second, b_second)


def solution(mesh):
    both = ("inner", "outer")
    in_specs = (
        P(both, None),
        P(both, None, None, None),
        P(both, None),
        P(both),
        P(both),
        P(both, None),
        P(both, None, None),
        P(both, None),
        P(both, None, None),
        P(both, None),
        P(),
        P(),
        P(),
        P(),
        P(),
    )
    sizes = (mesh.shape["inner"], mesh.shape["outer"])
    return jax.shard_map(
        functools.partial(local, sizes),
        mesh=mesh,
        in_specs=in_specs,
        out_specs=P(both, None),
        check_vma=False,
    )
```

time: 224 us -> 79.8 us (0.36)
  Pallas kernels: 0 us -> 66.7 us
  matrix products: 49.6 us -> 0 us
  waiting for transfers between devices: 46.4 us -> 0 us
  local copies, waits for them, and re-layouts: 56.8 us -> 11.2 us
  blocking collectives: 36.8 us -> 0 us
  other arithmetic: 21.8 us -> 0 us
  starting transfers between devices: 10 us -> 0 us
    pallas_call x0 -> x4, Pallas kernels: none -> 66.7 us  [the longest x1 30.4 us: exchange(): pl.pallas_call(functools.partial(exchange_kernel, n_inner, n_outer), out_...]
    gather x15 -> x0, local copies, waits for them, and re-layouts: 55.4 us -> none  [the longest x8 47.4 us: aggregate(): gathered = table[source_group]]
    dot_general x10 -> x0, matrix products: 49.6 us -> none  [the longest x8 37.1 us: aggregate(): jnp.einsum('bjrk,bjkf->brf', tile_group, gathered, preferred_element_type...]
    all_to_all x2 -> x0, waiting for transfers between devices: 46.4 us -> none  [the longest x1 26.5 us: local(): lax.all_to_all(packed(blocks, border, send_outer[0], count_outer[0], capa...]
    psum x1 -> x0, blocking collectives: 36.8 us -> none  [local(): lax.psum((count_local, jnp.sum(masked, axis=0), jnp.sum(masked * masked,...]
    unnamed x20 -> x28, local copies, waits for them, and re-layouts: 0.06 us -> 11.2 us
    all_to_all x2 -> x0, starting transfers between devices: 10 us -> none  [the longest x1 6.32 us: local(): lax.all_to_all(packed(blocks, border, send_inner[0], count_inner[0], capa...]
    select_n x16 -> x0, other arithmetic: 8.64 us -> none  [the longest x1 5.23 us: local(): features_live = jnp.where(live[:, None], features, zero_bf)]
  transfers between devices with their start and end apart: 2 -> 0, of which waited for: 2 -> 0; matrix products, arithmetic and copies ran while one was open for 3% -> 0% of each run, Pallas kernels for 0% -> 0%
where the time goes in v1:
time: 79.8 us; the launch traced here: 78.6 us
  Pallas kernels  66.7 us (84%)
  local copies, waits for them, and re-layouts  11.2 us (14%)
    pallas_call x1, Pallas kernels, exchange(): pl.pallas_call(functools.partial(exchange_kernel, n_inner, n_outer), out_...  30.4 us
    pallas_call x1, Pallas kernels, remote_tiles(): pl.pallas_call(remote_kernel, grid_spec=pltpu.PrefetchScalarGridSpec(num_...  19 us
    pallas_call x1, Pallas kernels, all_totals(): pl.pallas_call(functools.partial(totals_kernel, n_inner, n_outer), out_sh...  11.3 us
    unnamed x28, local copies, waits for them, and re-layouts  11.2 us
    pallas_call x1, Pallas kernels, finish(): pl.pallas_call(finish_kernel, grid_spec=pltpu.PrefetchScalarGridSpec(num_...  5.91 us

profile of v1, /device:TPU:0, one launch (start us, length us, event | category | flops | bytes accessed | tf_op | source)
XLA Modules:
  0.0 78.6 jit_solution(16572656040500072576)
XLA Ops:
  0.7 0.8 copy.15.send_out_ref
  1.4 0.8 copy.16.src_ref
  2.2 0.0 copy-start.2
  2.2 2.2 %copy-done.2 = bf16[8192,256]{1,0:T(8,128)(2,1)S(1)} copy-done((bf16[8192,256]{1,0:T(8,128)(2,1)S(1)}, bf16[8192,256]{1,0:T(8,128)(2,1)}, u32[]{:S(2)}) %copy-start.2) | copy-done | bytes 4194328
  4.4 0.0 copy-start.7
  4.4 0.7 copy-done.7
  5.0 0.0 copy-start.8
  5.0 0.7 copy-done.8
  5.7 0.0 copy-start.12
  5.7 0.7 copy-done.12
  6.4 0.0 copy-start.3
  6.4 30.4 %shard_map.127 = (bf16[49,128,256]{2,1,0:T(8,128)(2,1)S(1)}, f32[64,128,256]{2,1,0:T(8,128)}) custom-call(s32[64,8]{1,0:T(8,128)S(1)} %copy.16.src_ref, s32[64]{0:T(128)S(1)} %copy-done.7, s32[1]{0:T(128)S(6)} %copy.17.node_ref, s32[1,8]{1,0:T(1,128)S(1)} %copy-done.12, s32[1,4,4]{2,1,0:T(4,128)S(1)} %copy-done.8, s32[1,8,4]{2,1,0:T(8,128)S(1)} %copy.15.send_out_ref, ...), custom_call_target="tpu_custom_call" | custom-call | tf_op jit(solution)/shard_map/pallas_call | solution.py:166
  36.8 0.0 copy-done.3
  36.8 0.0 copy-start.4
  36.8 0.0 copy-start.9
  36.8 0.0 copy-start.10
  36.8 0.0 copy-start.11
  36.8 19.0 %shard_map.128 = (bf16[8192,256]{1,0:T(8,128)(2,1)S(1)}, f32[8,256]{1,0:T(8,128)S(1)}) custom-call(s32[64,8]{1,0:T(8,128)S(1)} %copy.16.src_ref, s32[64]{0:T(128)S(1)} %copy-done.7, s32[1]{0:T(128)S(6)} %copy.17.node_ref, bf16[49,128,256]{2,1,0:T(8,128)(2,1)S(1)} %get-tuple-element.9.recv_ref, bf16[64,8,128,128]{3,2,1,0:T(8,128)(2,1)} %tile_ref.3, ...), custom_call_target="tpu_custom_call" | custom-call | tf_op jit(solution)/shard_map/pallas_call | solution.py:257
  55.9 0.0 copy-start
  55.9 2.0 %copy-done = bf16[8192,256]{1,0:T(8,128)(2,1)} copy-done((bf16[8192,256]{1,0:T(8,128)(2,1)}, bf16[8192,256]{1,0:T(8,128)(2,1)S(1)}, u32[]{:S(2)}) %copy-start) | copy-done | bytes 4194328
  57.9 0.0 copy-start.6
  57.9 0.6 copy-done.6
  58.5 11.3 %shard_map.129.totals_ref = f32[8,256]{1,0:T(8,128)} custom-call(f32[8,256]{1,0:T(8,128)} %copy-done.6), custom_call_target="tpu_custom_call" | custom-call | tf_op jit(solution)/shard_map/pallas_call | solution.py:312
  69.8 0.0 copy-done.4
  69.8 0.0 copy-done.9
  69.8 0.0 copy-done.10
  69.8 0.0 copy-done.11
  69.8 0.0 copy-start.1
  69.8 2.2 %copy-done.1 = bf16[8192,256]{1,0:T(8,128)(2,1)S(1)} copy-done((bf16[8192,256]{1,0:T(8,128)(2,1)S(1)}, bf16[8192,256]{1,0:T(8,128)(2,1)}, u32[]{:S(2)}) %copy-start.1) | copy-done | bytes 4194328
  72.0 0.0 copy-start.5
  72.0 0.7 copy-done.5
  72.7 5.9 %shard_map.130 = bf16[8192,256]{1,0:T(8,128)(2,1)} custom-call(s32[1]{0:T(128)S(6)} %copy.17.node_ref, f32[8,256]{1,0:T(8,128)S(1)} %copy-done.5, bf16[8192,256]{1,0:T(8,128)(2,1)S(1)} %copy-done.1, bf16[256,256]{1,0:T(8,128)(2,1)S(1)} %copy-done.3, f32[1,256]{1,0:T(1,128)S(1)} %bitcast.5, f32[1,256]{1,0:T(1,128)S(1)} %bitcast.6, ...), custom_call_target="tpu_custom_call" | custom-call | tf_op jit(solution)/shard_map/pallas_call | solution.py:350
Async XLA Ops:
  2.2 2.2 %copy-start.2 = (bf16[8192,256]{1,0:T(8,128)(2,1)S(1)}, bf16[8192,256]{1,0:T(8,128)(2,1)}, u32[]{:S(2)}) copy-start(bf16[8192,256]{1,0:T(8,128)(2,1)} %param.15) | copy-start | bytes 12582916
  4.4 0.7 copy-start.7
  5.0 0.7 copy-start.8
  5.7 0.7 copy-start.12
  6.4 30.4 %copy-start.3 = (bf16[256,256]{1,0:T(8,128)(2,1)S(1)}, bf16[256,256]{1,0:T(8,128)(2,1)}, u32[]{:S(2)}) copy-start(bf16[256,256]{1,0:T(8,128)(2,1)} %w1_ref.1) | copy-start | bytes 393220
  36.8 33.0 %copy-start.4 = (bf16[256,256]{1,0:T(8,128)(2,1)S(1)}, bf16[256,256]{1,0:T(8,128)(2,1)}, u32[]{:S(2)}) copy-start(bf16[256,256]{1,0:T(8,128)(2,1)} %w2_ref.1) | copy-start | bytes 393220
  36.8 33.0 %copy-start.9 = (f32[256]{0:T(256)S(1)}, f32[256]{0:T(256)}, u32[]{:S(2)}) copy-start(f32[256]{0:T(256)} %param.24) | copy-start | bytes 3076
  36.8 33.0 %copy-start.10 = (f32[256]{0:T(256)S(1)}, f32[256]{0:T(256)}, u32[]{:S(2)}) copy-start(f32[256]{0:T(256)} %param.25) | copy-start | bytes 3076
  36.8 33.0 %copy-start.11 = (f32[256]{0:T(256)S(1)}, f32[256]{0:T(256)}, u32[]{:S(2)}) copy-start(f32[256]{0:T(256)} %param.27) | copy-start | bytes 3076
  55.9 2.0 %copy-start = (bf16[8192,256]{1,0:T(8,128)(2,1)}, bf16[8192,256]{1,0:T(8,128)(2,1)S(1)}, u32[]{:S(2)}) copy-start(bf16[8192,256]{1,0:T(8,128)(2,1)S(1)} %get-tuple-element.12.combined_ref) | copy-start | bytes 12582916
  57.9 0.6 copy-start.6
  69.8 2.2 %copy-start.1 = (bf16[8192,256]{1,0:T(8,128)(2,1)S(1)}, bf16[8192,256]{1,0:T(8,128)(2,1)}, u32[]{:S(2)}) copy-start(bf16[8192,256]{1,0:T(8,128)(2,1)} %copy-done) | copy-start | bytes 12582916
  72.0 0.7 copy-start.5

commit v2 on v1

--- a/solution.py
+++ b/solution.py
@@ -12,7 +12,7 @@
 BF16 = jnp.bfloat16
 F32 = jnp.float32
 DEPTH = 4
-GROUP = 4
+GROUP = 8
 
 
 def peers_of(n_inner, n_outer):
@@ -32,22 +32,29 @@
 def exchange_kernel(
     n_inner,
     n_outer,
-    src_ref,
-    count_ref,
     node_ref,
-    border_ref,
-    send_in_ref,
-    send_out_ref,
+    src_hbm,
+    count_hbm,
+    border_hbm,
+    send_in_hbm,
+    send_out_hbm,
     feat_ref,
     tile_ref,
     recv_ref,
     part_ref,
     table,
+    masks,
     packed,
     tile_buf,
     part_buf,
+    src_ref,
+    count_ref,
+    border_ref,
+    send_in_ref,
+    send_out_ref,
     feat_sem,
     zero_sem,
+    list_sem,
     tile_sem,
     part_sem,
     send_sem,
@@ -59,26 +66,49 @@
     i, o = lax.axis_index("inner"), lax.axis_index("outer")
     inner, outer = peers_of(n_inner, n_outer)
     filled = node_ref[0]
-    row_ids = lax.broadcasted_iota(jnp.int32, (rows, width), 0)
-
+    steps = nb // DEPTH
+
+    lists = [
+        pltpu.make_async_copy(source, target, list_sem.at[at])
+        for at, (source, target) in enumerate(
+            (
+                (border_hbm, border_ref),
+                (send_in_hbm, send_in_ref),
+                (send_out_hbm, send_out_ref),
+                (src_hbm, src_ref),
+                (count_hbm, count_ref),
+            )
+        )
+    ]
+    for copy in lists:
+        copy.start()
     feats = pltpu.make_async_copy(feat_ref, table.at[pl.ds(0, nb)], feat_sem)
     feats.start()
 
-    def tile_copy(b, slot):
-        return pltpu.make_async_copy(tile_ref.at[b], tile_buf.at[slot], tile_sem.at[slot])
-
-    def part_copy(b, slot):
-        return pltpu.make_async_copy(part_buf.at[slot], part_ref.at[b], part_sem.at[slot])
-
-    for d in range(DEPTH):
-        tile_copy(d, d).start()
+    def tile_copy(g, slot):
+        return pltpu.make_async_copy(
+            tile_ref.at[pl.ds(g * DEPTH, DEPTH)], tile_buf.at[slot], tile_sem.at[slot]
+        )
+
+    def part_copy(g, slot):
+        return pltpu.make_async_copy(
+            part_buf.at[slot], part_ref.at[pl.ds(g * DEPTH, DEPTH)], part_sem.at[slot]
+        )
+
+    row_ids = lax.broadcasted_iota(jnp.int32, (rows, width), 0)
+    masks[0] = jnp.ones((rows, width), BF16)
+    masks[1] = jnp.where(row_ids < lax.rem(filled, rows), 1.0, 0.0).astype(BF16)
+    masks[2] = jnp.zeros((rows, width), BF16)
+    table[nb] = jnp.zeros((rows, width), BF16)
     enter(inner + outer)
+    for copy in lists:
+        copy.wait()
     feats.wait()
-    table[nb] = jnp.zeros((rows, width), BF16)
 
     def live_block(block):
-        data = table[block].astype(F32)
-        return jnp.where(row_ids < filled - block * rows, data, 0.0).astype(BF16)
+        above = (block * rows >= filled).astype(jnp.int32)
+        partly = (block * rows + rows > filled).astype(jnp.int32)
+        return table[block] * masks[above + partly]
 
     copies = []
     order = []
@@ -92,7 +122,7 @@
             if is_inner:
                 entry = send_in_ref[0, device[0], c]
             else:
-                entry = send_out_ref[0, device[1], c]
+                entry = send_out_ref[0, c, device[1]]
             packed[at, c] = live_block(border_ref[0, entry])
         first_slot = i * cap if is_inner else (n_inner + o) * cap
         copy = pltpu.make_async_remote_copy(
@@ -106,49 +136,52 @@
         copy.start()
         copies.append(copy)
 
-    @pl.loop(0, nb)
-    def _(block):
-        table[block] = live_block(block)
+    for g in range(2):
+        tile_copy(g, g).start()
+
+    @pl.loop(0, nb // 4)
+    def _(at):
+        for d in range(4):
+            table[at * 4 + d] = live_block(at * 4 + d)
 
     last = recv_ref.shape[0] - 1
     zeros = pltpu.make_async_copy(table.at[nb], recv_ref.at[last], zero_sem)
     zeros.start()
 
-    def one(b, slot, wait_part, more):
-        tile_copy(b, slot).wait()
-        used = count_ref[b]
-        total = table[b].astype(F32)
-        for pair in range(per_block // 2):
-            weights, sources = [], []
-            for j in (2 * pair, 2 * pair + 1):
-                s = src_ref[b, j]
-                ok = jnp.logical_and(s < nb, j < used)
-                sources.append(table[jnp.where(ok, s, nb)])
-                weights.append(tile_buf[slot, j])
-            total += jnp.dot(
-                jnp.concatenate(weights, axis=1),
-                jnp.concatenate(sources, axis=0),
-                preferred_element_type=F32,
-            )
-        if wait_part:
-            part_copy(b - DEPTH, slot).wait()
-        part_buf[slot] = total
-        part_copy(b, slot).start()
-        if more:
-            tile_copy(b + DEPTH, slot).start()
-
-    for d in range(DEPTH):
-        one(d, d, False, True)
-
-    @pl.loop(1, nb // DEPTH - 1)
+    @pl.loop(0, steps)
     def _(g):
+        slot = lax.rem(g, 2)
+        tile_copy(g, slot).wait()
+
+        @pl.when(g >= 2)
+        def _():
+            part_copy(g - 2, slot).wait()
+
         for d in range(DEPTH):
-            one(g * DEPTH + d, d, True, True)
-
-    for d in range(DEPTH):
-        one(nb - DEPTH + d, d, True, False)
-    for d in range(DEPTH):
-        part_copy(nb - DEPTH + d, d).wait()
+            b = g * DEPTH + d
+            used = count_ref[b]
+            total = table[b].astype(F32)
+            for pair in range(per_block // 2):
+                weights, sources = [], []
+                for j in (2 * pair, 2 * pair + 1):
+                    s = src_ref[j, b]
+                    ok = jnp.logical_and(s < nb, j < used)
+                    sources.append(table[jnp.where(ok, s, nb)])
+                    weights.append(tile_buf[slot, d, j])
+                total += jnp.dot(
+                    jnp.concatenate(weights, axis=1),
+                    jnp.concatenate(sources, axis=0),
+                    preferred_element_type=F32,
+                )
+            part_buf[slot, d] = total
+        part_copy(g, slot).start()
+
+        @pl.when(g + 2 < steps)
+        def _():
+            tile_copy(g + 2, slot).start()
+
+    for g in (steps - 2, steps - 1):
+        part_copy(g, g % 2).wait()
     zeros.wait()
     for copy in copies:
         copy.wait()
@@ -162,38 +195,52 @@
     slots = (n_inner + n_outer) * cap + 1
     partners = n_inner + n_outer - 2
     smem = pl.BlockSpec(memory_space=pltpu.SMEM)
-    hbm = pl.BlockSpec(memory_space=pl.ANY)
+    hbm = pl.BlockSpec(memory_space=pltpu.HBM)
+    free = pl.BlockSpec(memory_space=pl.ANY)
     return pl.pallas_call(
         functools.partial(exchange_kernel, n_inner, n_outer),
         out_shape=(
             jax.ShapeDtypeStruct((slots, rows, width), BF16),
             jax.ShapeDtypeStruct((nb, rows, width), F32),
         ),
-        in_specs=[smem] * 6 + [hbm] * 2,
-        out_specs=(hbm, hbm),
+        in_specs=[smem] + [hbm] * 7,
+        out_specs=(free, free),
         scratch_shapes=[
             pltpu.VMEM((nb + 1, rows, width), BF16),
+            pltpu.VMEM((3, rows, width), BF16),
             pltpu.VMEM((partners, cap, rows, width), BF16),
-            pltpu.VMEM((DEPTH, per_block, rows, rows), BF16),
-            pltpu.VMEM((DEPTH, rows, width), F32),
+            pltpu.VMEM((2, DEPTH, per_block, rows, rows), BF16),
+            pltpu.VMEM((2, DEPTH, rows, width), F32),
+            pltpu.SMEM(tile_src.shape, jnp.int32),
+            pltpu.SMEM(tile_count.shape, jnp.int32),
+            pltpu.SMEM(boundary.shape, jnp.int32),
+            pltpu.SMEM(send_inner.shape, jnp.int32),
+            pltpu.SMEM(send_outer.shape, jnp.int32),
             pltpu.SemaphoreType.DMA,
             pltpu.SemaphoreType.DMA,
-            pltpu.SemaphoreType.DMA((DEPTH,)),
-            pltpu.SemaphoreType.DMA((DEPTH,)),
+            pltpu.SemaphoreType.DMA((5,)),
+            pltpu.SemaphoreType.DMA((2,)),
+            pltpu.SemaphoreType.DMA((2,)),
             pltpu.SemaphoreType.DMA((partners,)),
             pltpu.SemaphoreType.DMA((partners,)),
         ],
         compiler_params=pltpu.CompilerParams(
-            collective_id=0, has_side_effects=True, vmem_limit_bytes=40 << 20
+            collective_id=0, has_side_effects=True, vmem_limit_bytes=18 << 20
         ),
-    )(tile_src, tile_count, node_count, boundary, send_inner, send_outer, blocks, tiles)
+    )(
+        node_count,
+        *(
+            pltpu.with_memory_space_constraint(x, pltpu.HBM)
+            for x in (tile_src, tile_count, boundary, send_inner, send_outer, blocks, tiles)
+        ),
+    )
 
 
 def remote_kernel(
     src_ref, count_ref, node_ref, recv_ref, tile_ref, part_ref, w_ref, out_ref, stats_ref
 ):
     step = pl.program_id(0)
-    nb_all = src_ref.shape[0]
+    nb_all = src_ref.shape[1]
     group, per_block, rows = tile_ref.shape[:3]
     width = part_ref.shape[2]
     zero_slot = recv_ref.shape[0] - 1
@@ -209,7 +256,7 @@
         used = count_ref[b]
         code, n = jnp.int32(0), jnp.int32(0)
         for j in range(per_block):
-            hit = jnp.logical_and(src_ref[b, j] >= nb_all, j < used).astype(jnp.int32)
+            hit = jnp.logical_and(src_ref[j, b] >= nb_all, j < used).astype(jnp.int32)
             code = code + hit * jnp.left_shift(jnp.int32(j), 3 * n)
             n = n + hit
         found.append((b, code, n))
@@ -219,7 +266,7 @@
         weights, sources = [], []
         for rank in (2 * pair, 2 * pair + 1):
             j = jnp.bitwise_and(jnp.right_shift(code, 3 * rank), 7)
-            slot = jnp.where(rank < n, src_ref[b, j] - nb_all, zero_slot)
+            slot = jnp.where(rank < n, src_ref[j, b] - nb_all, zero_slot)
             sources.append(recv_ref[slot])
             weights.append(tile_ref[g, j])
         return jnp.dot(
@@ -240,20 +287,35 @@
     combined = part_ref[...].reshape(group * rows, width).astype(BF16)
     out_ref[...] = combined
     first = jnp.dot(combined, w_ref[...], preferred_element_type=F32)
-    row_ids = lax.broadcasted_iota(jnp.int32, first.shape, 0)
-    kept = jnp.where(row_ids < filled - step * group * rows, first, 0.0)
-    stats_ref[0:1, :] += jnp.sum(kept, axis=0, keepdims=True)
-    stats_ref[1:2, :] += jnp.sum(kept * kept, axis=0, keepdims=True)
+    halves = first.shape[1] // 128
+    rows_left = filled - step * group * rows
+
+    def add_sums(kept):
+        for at, value in enumerate((kept, kept * kept)):
+            line = jnp.sum(value, axis=0, keepdims=True)
+            for h in range(halves):
+                spot = at * halves + h
+                stats_ref[spot : spot + 1, :] += line[:, h * 128 : (h + 1) * 128]
+
+    @pl.when(rows_left >= group * rows)
+    def _():
+        add_sums(first)
+
+    @pl.when(jnp.logical_and(rows_left > 0, rows_left < group * rows))
+    def _():
+        row_ids = lax.broadcasted_iota(jnp.int32, first.shape, 0)
+        add_sums(jnp.where(row_ids < rows_left, first, 0.0))
 
     @pl.when(step == 0)
     def _():
-        stats_ref[2:3, :] = jnp.full((1, stats_ref.shape[1]), filled.astype(F32))
+        spot = 2 * halves
+        stats_ref[spot : spot + 1, :] = jnp.full((1, 128), filled.astype(F32))
 
 
 def remote_tiles(tile_src, tile_count, node_count, recv, tiles, part, w_first):
     nb, per_block, rows = tiles.shape[:3]
     width = part.shape[2]
-    hidden = w_first.shape[1]
+    lines = -(-(2 * (w_first.shape[1] // 128) + 1) // 8) * 8
     return pl.pallas_call(
         remote_kernel,
         grid_spec=pltpu.PrefetchScalarGridSpec(
@@ -267,14 +329,14 @@
             ],
             out_specs=[
                 pl.BlockSpec((GROUP * rows, width), lambda s, *_: (s, 0)),
-                pl.BlockSpec((8, hidden), lambda s, *_: (0, 0)),
+                pl.BlockSpec((lines, 128), lambda s, *_: (0, 0)),
             ],
         ),
         out_shape=(
             jax.ShapeDtypeStruct((nb * rows, width), BF16),
-            jax.ShapeDtypeStruct((8, hidden), F32),
+            jax.ShapeDtypeStruct((lines, 128), F32),
         ),
-        compiler_params=pltpu.CompilerParams(vmem_limit_bytes=40 << 20),
+        compiler_params=pltpu.CompilerParams(vmem_limit_bytes=20 << 20),
     )(tile_src, tile_count, node_count, recv, tiles, part, w_first)
 
 
@@ -321,7 +383,7 @@
             pltpu.SemaphoreType.DMA((partners,)),
             pltpu.SemaphoreType.DMA((partners,)),
         ],
-        compiler_params=pltpu.CompilerParams(collective_id=1, has_side_effects=True),
+        compiler_params=pltpu.CompilerParams(collective_id=1, has_side_effects=True, vmem_limit_bytes=2 << 20),
     )(stats)
 
 
@@ -330,16 +392,32 @@
 ):
     rows = out_ref.shape[0]
     filled = node_ref[0]
-    count = totals_ref[2:3, :]
-    mean = totals_ref[0:1, :] / count
-    variance = totals_ref[1:2, :] / count - mean * mean
+    halves = gamma_ref.shape[1] // 128
+
+    def line(first_row):
+        parts = [totals_ref[first_row + h : first_row + h + 1, :] for h in range(halves)]
+        return jnp.concatenate(parts, axis=1)
+
+    count = totals_ref[2 * halves : 2 * halves + 1, 0:1]
+    mean = line(0) / count
+    variance = line(halves) / count - mean * mean
     scale = gamma_ref[...] * lax.rsqrt(variance + EPSILON)
-    first = jnp.dot(combined_ref[...], w1_ref[...], preferred_element_type=F32)
-    normed = jnp.maximum(scale * (first - mean) + beta_ref[...], 0.0).astype(BF16)
-    output = jnp.dot(normed, w2_ref[...], preferred_element_type=F32) + bias_ref[...]
-    row_ids = lax.broadcasted_iota(jnp.int32, output.shape, 0)
-    live = row_ids < filled - pl.program_id(0) * rows
-    out_ref[...] = jnp.where(live, output, 0.0).astype(BF16)
+    rows_left = filled - pl.program_id(0) * rows
+
+    def result():
+        first = jnp.dot(combined_ref[...], w1_ref[...], preferred_element_type=F32)
+        normed = jnp.maximum(scale * (first - mean) + beta_ref[...], 0.0).astype(BF16)
+        return jnp.dot(normed, w2_ref[...], preferred_element_type=F32) + bias_ref[...]
+
+    @pl.when(rows_left >= rows)
+    def _():
+        out_ref[...] = result().astype(BF16)
+
+    @pl.when(rows_left < rows)
+    def _():
+        output = result()
+        row_ids = lax.broadcasted_iota(jnp.int32, output.shape, 0)
+        out_ref[...] = jnp.where(row_ids < rows_left, output, 0.0).astype(BF16)
 
 
 def finish(node_count, totals, combined, w_first, gamma, beta, w_second, b_second):
@@ -364,7 +442,7 @@
             out_specs=pl.BlockSpec((rows, width), lambda s, *_: (s, 0)),
         ),
         out_shape=jax.ShapeDtypeStruct((nodes, width), BF16),
-        compiler_params=pltpu.CompilerParams(vmem_limit_bytes=40 << 20),
+        compiler_params=pltpu.CompilerParams(vmem_limit_bytes=20 << 20),
     )(
         node_count,
         totals,
@@ -397,6 +475,9 @@
 ):
     nblocks, _, rows = tiles.shape[:3]
     blocks = features.reshape(nblocks, rows, features.shape[1])
+    tile_src = tile_src.T
+    send_outer = send_outer.transpose(0, 2, 1)
+    tiles = pltpu.with_memory_space_constraint(tiles, pltpu.HBM)
     recv, part = exchange(
         mesh_sizes, tile_src, tile_count, node_count, boundary, send_inner, send_outer, blocks, tiles
     )

time: 79.8 us -> 59.9 us (0.75)
  local copies, waits for them, and re-layouts: 11.2 us -> 0.04 us
  Pallas kernels: 66.7 us -> 58.4 us
    unnamed x28 -> x14, local copies, waits for them, and re-layouts: 11.2 us -> 0.04 us
    pallas_call x1, Pallas kernels: 19 us -> 13 us  [remote_tiles(): pl.pallas_call(remote_kernel, grid_spec=pltpu.PrefetchScalarGridSpec(num_...]
    pallas_call x1, Pallas kernels: 30.4 us -> 28.1 us  [exchange(): pl.pallas_call(functools.partial(exchange_kernel, n_inner, n_outer), out_...]
where the time goes in v2:
time: 59.9 us; the launch traced here: 59.2 us
  Pallas kernels  58.4 us (97%)
  between operations  0.79 us (1%)
    pallas_call x1, Pallas kernels, exchange(): pl.pallas_call(functools.partial(exchange_kernel, n_inner, n_outer), out_...  28.1 us
    pallas_call x1, Pallas kernels, remote_tiles(): pl.pallas_call(remote_kernel, grid_spec=pltpu.PrefetchScalarGridSpec(num_...  13 us
    pallas_call x1, Pallas kernels, all_totals(): pl.pallas_call(functools.partial(totals_kernel, n_inner, n_outer), out_sh...  11 us
    pallas_call x1, Pallas kernels, finish(): pl.pallas_call(finish_kernel, grid_spec=pltpu.PrefetchScalarGridSpec(num_...  6.33 us

profile of v2, /device:TPU:0, one launch (start us, length us, event | category | flops | bytes accessed | tf_op | source)
XLA Modules:
  0.0 59.2 jit_solution(15102646505102138200)
XLA Ops:
  0.7 0.0 copy-start
  0.7 0.0 copy-start.2
  0.7 0.0 copy-start.3
  0.7 28.1 %shard_map.127 = (bf16[49,128,256]{2,1,0:T(8,128)(2,1)S(1)}, f32[64,128,256]{2,1,0:T(8,128)S(1)}) custom-call(s32[1]{0:T(128)S(6)} %copy.14.node_ref, s32[8,64]{1,0:T(8,128)} %bitcast.6, s32[64]{0:T(128)} %count_ref.1, s32[1,8]{1,0:T(1,128)} %border_hbm.1, s32[1,4,4]{2,1,0:T(4,128)} %send_in_hbm.1, s32[1,4,8]{2,1,0:T(4,128)} %bitcast.12, ...), custom_call_target="tpu_custom_call" | custom-call | tf_op jit(solution)/shard_map/pallas_call | solution.py:200
  28.8 0.0 copy-done
  28.8 0.0 copy-done.2
  28.8 0.0 copy-done.3
  28.8 0.0 copy-start.1
  28.8 0.0 copy-start.4
  28.8 0.0 copy-start.5
  28.8 0.0 copy-start.6
  28.8 13.0 %shard_map.128 = (bf16[8192,256]{1,0:T(8,128)(2,1)S(1)}, f32[8,128]{1,0:T(8,128)S(1)}) custom-call(s32[8,64]{1,0:T(8,128)S(1)} %bitcast.7, s32[64]{0:T(128)S(1)} %copy-done.3, s32[1]{0:T(128)S(6)} %copy.14.node_ref, bf16[49,128,256]{2,1,0:T(8,128)(2,1)S(1)} %get-tuple-element.9.recv_ref, bf16[64,8,128,128]{3,2,1,0:T(8,128)(2,1)} %tile_ref.3, ...), custom_call_target="tpu_custom_call" | custom-call | tf_op jit(solution)/shard_map/pallas_call | solution.py:319
  41.8 11.0 %shard_map.129.totals_ref = f32[8,128]{1,0:T(8,128)S(1)} custom-call(f32[8,128]{1,0:T(8,128)S(1)} %get-tuple-element.11.stats_ref), custom_call_target="tpu_custom_call" | custom-call | tf_op jit(solution)/shard_map/pallas_call | solution.py:374
  52.8 0.0 copy-done.1
  52.9 0.0 copy-done.4
  52.9 0.0 copy-done.5
  52.9 0.0 copy-done.6
  52.9 6.3 %shard_map.130 = bf16[8192,256]{1,0:T(8,128)(2,1)} custom-call(s32[1]{0:T(128)S(6)} %copy.14.node_ref, f32[8,128]{1,0:T(8,128)S(1)} %shard_map.129.totals_ref, bf16[8192,256]{1,0:T(8,128)(2,1)S(1)} %get-tuple-element.12.combined_ref, bf16[256,256]{1,0:T(8,128)(2,1)S(1)} %copy-done, f32[1,256]{1,0:T(1,128)S(1)} %bitcast.8, f32[1,256]{1,0:T(1,128)S(1)} %bitcast.9, ...), custom_call_target="tpu_custom_call" | custom-call | tf_op jit(solution)/shard_map/pallas_call | solution.py:428
Async XLA Ops:
  0.7 28.1 %copy-start = (bf16[256,256]{1,0:T(8,128)(2,1)S(1)}, bf16[256,256]{1,0:T(8,128)(2,1)}, u32[]{:S(2)}) copy-start(bf16[256,256]{1,0:T(8,128)(2,1)} %w1_ref.1) | copy-start | bytes 393220
  0.7 28.1 %copy-start.2 = (s32[64,8]{0,1:T(8,128)S(1)}, s32[64,8]{0,1:T(8,128)}, u32[]{:S(2)}) copy-start(s32[64,8]{0,1:T(8,128)} %param.17) | copy-start | bytes 6148
  0.7 28.1 %copy-start.3 = (s32[64]{0:T(128)S(1)}, s32[64]{0:T(128)}, u32[]{:S(2)}) copy-start(s32[64]{0:T(128)} %count_ref.1) | copy-start | bytes 772
  28.8 24.1 %copy-start.1 = (bf16[256,256]{1,0:T(8,128)(2,1)S(1)}, bf16[256,256]{1,0:T(8,128)(2,1)}, u32[]{:S(2)}) copy-start(bf16[256,256]{1,0:T(8,128)(2,1)} %w2_ref.1) | copy-start | bytes 393220
  28.8 24.1 %copy-start.4 = (f32[256]{0:T(256)S(1)}, f32[256]{0:T(256)}, u32[]{:S(2)}) copy-start(f32[256]{0:T(256)} %param.24) | copy-start | bytes 3076
  28.8 24.1 %copy-start.5 = (f32[256]{0:T(256)S(1)}, f32[256]{0:T(256)}, u32[]{:S(2)}) copy-start(f32[256]{0:T(256)} %param.25) | copy-start | bytes 3076
  28.8 24.1 %copy-start.6 = (f32[256]{0:T(256)S(1)}, f32[256]{0:T(256)}, u32[]{:S(2)}) copy-start(f32[256]{0:T(256)} %param.27) | copy-start | bytes 3076

commit v3 on v2

--- a/solution.py
+++ b/solution.py
@@ -12,6 +12,9 @@
 BF16 = jnp.bfloat16
 F32 = jnp.float32
 DEPTH = 4
+BATCH = 4
+REMOTE_LIMIT = 32
+FINISH_LIMIT = 16
 GROUP = 8
 
 
@@ -237,107 +240,143 @@
 
 
 def remote_kernel(
-    src_ref, count_ref, node_ref, recv_ref, tile_ref, part_ref, w_ref, out_ref, stats_ref
+    src_ref,
+    count_ref,
+    node_ref,
+    recv_ref,
+    tile_hbm,
+    part_ref,
+    w_ref,
+    out_ref,
+    stats_ref,
+    tile_ref,
+    total_ref,
+    code_ref,
+    found_ref,
+    extra_ref,
+    tile_sem,
 ):
-    step = pl.program_id(0)
-    nb_all = src_ref.shape[1]
-    group, per_block, rows = tile_ref.shape[:3]
+    nb, per_block, rows = tile_ref.shape[:3]
     width = part_ref.shape[2]
     zero_slot = recv_ref.shape[0] - 1
     filled = node_ref[0]
-
-    @pl.when(step == 0)
-    def _():
-        stats_ref[...] = jnp.zeros_like(stats_ref)
-
-    found = []
-    for g in range(group):
-        b = step * group + g
-        used = count_ref[b]
-        code, n = jnp.int32(0), jnp.int32(0)
-        for j in range(per_block):
-            hit = jnp.logical_and(src_ref[j, b] >= nb_all, j < used).astype(jnp.int32)
-            code = code + hit * jnp.left_shift(jnp.int32(j), 3 * n)
-            n = n + hit
-        found.append((b, code, n))
-
-    def pair_product(g, pair):
-        b, code, n = found[g]
+    steps = nb // GROUP
+
+    def tile_copy(step):
+        some = pl.ds(step * GROUP, GROUP)
+        return pltpu.make_async_copy(tile_hbm.at[some], tile_ref.at[some], tile_sem.at[step])
+
+    for step in range(steps):
+        tile_copy(step).start()
+
+    def pair_product(b, code, n, pair):
         weights, sources = [], []
-        for rank in (2 * pair, 2 * pair + 1):
+        for at in range(2):
+            rank = 2 * pair + at
             j = jnp.bitwise_and(jnp.right_shift(code, 3 * rank), 7)
-            slot = jnp.where(rank < n, src_ref[j, b] - nb_all, zero_slot)
+            slot = jnp.where(rank < n, src_ref[j, b] - nb, zero_slot)
             sources.append(recv_ref[slot])
-            weights.append(tile_ref[g, j])
+            weights.append(tile_ref[b, j])
         return jnp.dot(
             jnp.concatenate(weights, axis=1),
             jnp.concatenate(sources, axis=0),
             preferred_element_type=F32,
         )
 
-    for g in range(group):
-        part_ref[g] += pair_product(g, 0)
-    for g in range(group):
-        for pair in range(1, per_block // 2):
-
-            @pl.when(found[g][2] > 2 * pair)
-            def _():
-                part_ref[g] += pair_product(g, pair)
-
-    combined = part_ref[...].reshape(group * rows, width).astype(BF16)
-    out_ref[...] = combined
-    first = jnp.dot(combined, w_ref[...], preferred_element_type=F32)
-    halves = first.shape[1] // 128
-    rows_left = filled - step * group * rows
-
-    def add_sums(kept):
-        for at, value in enumerate((kept, kept * kept)):
-            line = jnp.sum(value, axis=0, keepdims=True)
-            for h in range(halves):
-                spot = at * halves + h
-                stats_ref[spot : spot + 1, :] += line[:, h * 128 : (h + 1) * 128]
-
-    @pl.when(rows_left >= group * rows)
-    def _():
-        add_sums(first)
-
-    @pl.when(jnp.logical_and(rows_left > 0, rows_left < group * rows))
-    def _():
-        row_ids = lax.broadcasted_iota(jnp.int32, first.shape, 0)
-        add_sums(jnp.where(row_ids < rows_left, first, 0.0))
-
-    @pl.when(step == 0)
-    def _():
-        spot = 2 * halves
-        stats_ref[spot : spot + 1, :] = jnp.full((1, 128), filled.astype(F32))
+    def first_pairs(step, extra):
+        tile_copy(step).wait()
+        for g in range(GROUP):
+            b = step * GROUP + g
+            used = count_ref[b]
+            code, n = jnp.int32(0), jnp.int32(0)
+            for j in range(per_block):
+                hit = jnp.logical_and(src_ref[j, b] >= nb, j < used).astype(jnp.int32)
+                code = code + hit * jnp.left_shift(jnp.int32(j), 3 * n)
+                n = n + hit
+            code_ref[b] = code
+            found_ref[b] = n
+            for pair in range(1, per_block // 2):
+                extra_ref[extra] = b * 8 + pair
+                extra = extra + (n > 2 * pair).astype(jnp.int32)
+            total_ref[b] = part_ref[b] + pair_product(b, code, n, 0)
+        return extra
+
+    extra = lax.fori_loop(0, steps, first_pairs, jnp.int32(0))
+    for at in range(BATCH):
+        extra_ref[extra + at] = per_block // 2
+
+    @pl.loop(0, (extra + BATCH - 1) // BATCH)
+    def _(turn):
+        products = []
+        for at in range(BATCH):
+            item = extra_ref[turn * BATCH + at]
+            b = item // 8
+            products.append((b, pair_product(b, code_ref[b], found_ref[b], lax.rem(item, 8))))
+        for b, product in products:
+            total_ref[b] += product
+
+    halves = w_ref.shape[1] // 128
+    stats_ref[...] = jnp.zeros_like(stats_ref)
+    stats_ref[2 * halves : 2 * halves + 1, :] = jnp.full((1, 128), filled.astype(F32))
+
+    @pl.loop(0, steps)
+    def _(step):
+        blocks = pl.ds(step * GROUP, GROUP)
+        combined = total_ref[blocks].reshape(GROUP * rows, width).astype(BF16)
+        out_ref[pl.ds(step * (GROUP * rows), GROUP * rows)] = combined
+        first = jnp.dot(combined, w_ref[...], preferred_element_type=F32)
+        rows_left = filled - step * (GROUP * rows)
+
+        def add_sums(kept):
+            for at, value in enumerate((kept, kept * kept)):
+                line = jnp.sum(value, axis=0, keepdims=True)
+                for h in range(halves):
+                    spot = at * halves + h
+                    stats_ref[spot : spot + 1, :] += line[:, h * 128 : (h + 1) * 128]
+
+        @pl.when(rows_left >= GROUP * rows)
+        def _():
+            add_sums(first)
+
+        @pl.when(jnp.logical_and(rows_left > 0, rows_left < GROUP * rows))
+        def _():
+            row_ids = lax.broadcasted_iota(jnp.int32, first.shape, 0)
+            add_sums(jnp.where(row_ids < rows_left, first, 0.0))
 
 
 def remote_tiles(tile_src, tile_count, node_count, recv, tiles, part, w_first):
     nb, per_block, rows = tiles.shape[:3]
     width = part.shape[2]
     lines = -(-(2 * (w_first.shape[1] // 128) + 1) // 8) * 8
+    smem = pl.BlockSpec(memory_space=pltpu.SMEM)
+    vmem = pl.BlockSpec(memory_space=pltpu.VMEM)
+    hbm = pl.BlockSpec(memory_space=pltpu.HBM)
     return pl.pallas_call(
         remote_kernel,
-        grid_spec=pltpu.PrefetchScalarGridSpec(
-            num_scalar_prefetch=3,
-            grid=(nb // GROUP,),
-            in_specs=[
-                pl.BlockSpec(recv.shape, lambda s, *_: (0, 0, 0)),
-                pl.BlockSpec((GROUP, per_block, rows, rows), lambda s, *_: (s, 0, 0, 0)),
-                pl.BlockSpec((GROUP, rows, width), lambda s, *_: (s, 0, 0)),
-                pl.BlockSpec(w_first.shape, lambda s, *_: (0, 0)),
-            ],
-            out_specs=[
-                pl.BlockSpec((GROUP * rows, width), lambda s, *_: (s, 0)),
-                pl.BlockSpec((lines, 128), lambda s, *_: (0, 0)),
-            ],
-        ),
+        in_specs=[smem, smem, smem, vmem, hbm, vmem, vmem],
+        out_specs=(vmem, vmem),
         out_shape=(
             jax.ShapeDtypeStruct((nb * rows, width), BF16),
             jax.ShapeDtypeStruct((lines, 128), F32),
         ),
-        compiler_params=pltpu.CompilerParams(vmem_limit_bytes=20 << 20),
-    )(tile_src, tile_count, node_count, recv, tiles, part, w_first)
+        scratch_shapes=[
+            pltpu.VMEM(tiles.shape, BF16),
+            pltpu.VMEM((nb, rows, width), F32),
+            pltpu.SMEM((nb,), jnp.int32),
+            pltpu.SMEM((nb,), jnp.int32),
+            pltpu.SMEM((nb * per_block // 2 + BATCH,), jnp.int32),
+            pltpu.SemaphoreType.DMA((nb // GROUP,)),
+        ],
+        compiler_params=pltpu.CompilerParams(vmem_limit_bytes=REMOTE_LIMIT << 20),
+    )(
+        tile_src,
+        tile_count,
+        node_count,
+        recv,
+        pltpu.with_memory_space_constraint(tiles, pltpu.HBM),
+        part,
+        w_first,
+    )
 
 
 def totals_kernel(n_inner, n_outer, stats_ref, out_ref, first_buf, second_buf, mid, send_sem, recv_sem):
@@ -388,9 +427,20 @@
 
 
 def finish_kernel(
-    node_ref, totals_ref, combined_ref, w1_ref, gamma_ref, beta_ref, w2_ref, bias_ref, out_ref
+    node_ref,
+    totals_ref,
+    combined_ref,
+    w1_ref,
+    gamma_ref,
+    beta_ref,
+    w2_ref,
+    bias_ref,
+    out_hbm,
+    stage,
+    out_sem,
 ):
-    rows = out_ref.shape[0]
+    rows = stage.shape[1]
+    steps = out_hbm.shape[0] // rows
     filled = node_ref[0]
     halves = gamma_ref.shape[1] // 128
 
@@ -402,47 +452,59 @@
     mean = line(0) / count
     variance = line(halves) / count - mean * mean
     scale = gamma_ref[...] * lax.rsqrt(variance + EPSILON)
-    rows_left = filled - pl.program_id(0) * rows
-
-    def result():
-        first = jnp.dot(combined_ref[...], w1_ref[...], preferred_element_type=F32)
-        normed = jnp.maximum(scale * (first - mean) + beta_ref[...], 0.0).astype(BF16)
-        return jnp.dot(normed, w2_ref[...], preferred_element_type=F32) + bias_ref[...]
-
-    @pl.when(rows_left >= rows)
-    def _():
-        out_ref[...] = result().astype(BF16)
-
-    @pl.when(rows_left < rows)
-    def _():
-        output = result()
-        row_ids = lax.broadcasted_iota(jnp.int32, output.shape, 0)
-        out_ref[...] = jnp.where(row_ids < rows_left, output, 0.0).astype(BF16)
+
+    def out_copy(step, slot):
+        return pltpu.make_async_copy(
+            stage.at[slot], out_hbm.at[pl.ds(step * rows, rows)], out_sem.at[slot]
+        )
+
+    @pl.loop(0, steps)
+    def _(step):
+        slot = lax.rem(step, 2)
+        rows_left = filled - step * rows
+
+        @pl.when(step >= 2)
+        def _():
+            out_copy(step - 2, slot).wait()
+
+        def result():
+            combined = combined_ref[pl.ds(step * rows, rows)]
+            first = jnp.dot(combined, w1_ref[...], preferred_element_type=F32)
+            normed = jnp.maximum(scale * (first - mean) + beta_ref[...], 0.0).astype(BF16)
+            return jnp.dot(normed, w2_ref[...], preferred_element_type=F32) + bias_ref[...]
+
+        @pl.when(rows_left >= rows)
+        def _():
+            stage[slot] = result().astype(BF16)
+
+        @pl.when(jnp.logical_and(rows_left > 0, rows_left < rows))
+        def _():
+            output = result()
+            row_ids = lax.broadcasted_iota(jnp.int32, output.shape, 0)
+            stage[slot] = jnp.where(row_ids < rows_left, output, 0.0).astype(BF16)
+
+        @pl.when(rows_left <= 0)
+        def _():
+            stage[slot] = jnp.zeros(stage.shape[1:], BF16)
+
+        out_copy(step, slot).start()
+
+    for step in (steps - 2, steps - 1):
+        out_copy(step, step % 2).wait()
 
 
 def finish(node_count, totals, combined, w_first, gamma, beta, w_second, b_second):
     nodes, width = combined.shape
-    hidden = w_first.shape[1]
     rows = nodes // 8
-    whole = lambda s, *_: (0, 0)
+    smem = pl.BlockSpec(memory_space=pltpu.SMEM)
+    vmem = pl.BlockSpec(memory_space=pltpu.VMEM)
     return pl.pallas_call(
         finish_kernel,
-        grid_spec=pltpu.PrefetchScalarGridSpec(
-            num_scalar_prefetch=1,
-            grid=(nodes // rows,),
-            in_specs=[
-                pl.BlockSpec(totals.shape, whole),
-                pl.BlockSpec((rows, width), lambda s, *_: (s, 0)),
-                pl.BlockSpec(w_first.shape, whole),
-                pl.BlockSpec((1, hidden), whole),
-                pl.BlockSpec((1, hidden), whole),
-                pl.BlockSpec(w_second.shape, whole),
-                pl.BlockSpec((1, width), whole),
-            ],
-            out_specs=pl.BlockSpec((rows, width), lambda s, *_: (s, 0)),
-        ),
+        in_specs=[smem] + [vmem] * 7,
+        out_specs=pl.BlockSpec(memory_space=pltpu.HBM),
         out_shape=jax.ShapeDtypeStruct((nodes, width), BF16),
-        compiler_params=pltpu.CompilerParams(vmem_limit_bytes=20 << 20),
+        scratch_shapes=[pltpu.VMEM((2, rows, width), BF16), pltpu.SemaphoreType.DMA((2,))],
+        compiler_params=pltpu.CompilerParams(vmem_limit_bytes=FINISH_LIMIT << 20),
     )(
         node_count,
         totals,
@@ -477,7 +539,6 @@
     blocks = features.reshape(nblocks, rows, features.shape[1])
     tile_src = tile_src.T
     send_outer = send_outer.transpose(0, 2, 1)
-    tiles = pltpu.with_memory_space_constraint(tiles, pltpu.HBM)
     recv, part = exchange(
         mesh_sizes, tile_src, tile_count, node_count, boundary, send_inner, send_outer, blocks, tiles
     )

time: 59.9 us -> 55.9 us (0.933)
  Pallas kernels: 58.4 us -> 54.6 us
    pallas_call x2, Pallas kernels: 19.3 us -> 15.4 us  [the longest x1 10.8 us: remote_tiles(): pl.pallas_call(remote_kernel, in_specs=[smem, smem, smem, vmem, hbm, vmem...]
where the time goes in v3:
time: 55.9 us; the launch traced here: 55.4 us
  Pallas kernels  54.6 us (98%)
  between operations  0.79 us (1%)
    pallas_call x1, Pallas kernels, exchange(): pl.pallas_call(functools.partial(exchange_kernel, n_inner, n_outer), out_...  28.1 us
    pallas_call x1, Pallas kernels, all_totals(): pl.pallas_call(functools.partial(totals_kernel, n_inner, n_outer), out_sh...  11.1 us
    pallas_call x1, Pallas kernels, remote_tiles(): pl.pallas_call(remote_kernel, in_specs=[smem, smem, smem, vmem, hbm, vmem...  10.8 us
    pallas_call x1, Pallas kernels, finish(): pl.pallas_call(finish_kernel, in_specs=[smem] + [vmem] * 7, out_specs=pl....  4.62 us

profile of v3, /device:TPU:0, one launch (start us, length us, event | category | flops | bytes accessed | tf_op | source)
XLA Modules:
  0.0 55.4 jit_solution(3715464605867392396)
XLA Ops:
  0.7 0.0 copy-start
  0.7 0.0 copy-start.2
  0.7 0.0 copy-start.3
  0.7 28.1 %shard_map.127 = (bf16[49,128,256]{2,1,0:T(8,128)(2,1)S(1)}, f32[64,128,256]{2,1,0:T(8,128)S(1)}) custom-call(s32[1]{0:T(128)S(6)} %copy.14.node_ref, s32[8,64]{1,0:T(8,128)} %bitcast.6, s32[64]{0:T(128)} %count_ref.1, s32[1,8]{1,0:T(1,128)} %border_hbm.1, s32[1,4,4]{2,1,0:T(4,128)} %send_in_hbm.1, s32[1,4,8]{2,1,0:T(4,128)} %bitcast.12, ...), custom_call_target="tpu_custom_call" | custom-call | tf_op jit(solution)/shard_map/pallas_call | solution.py:203
  28.8 0.0 copy-done
  28.8 0.0 copy-done.2
  28.8 0.0 copy-done.3
  28.8 0.0 copy-start.1
  28.8 0.0 copy-start.4
  28.8 0.0 copy-start.5
  28.8 0.0 copy-start.6
  28.8 10.8 %shard_map.128 = (bf16[8192,256]{1,0:T(8,128)(2,1)S(1)}, f32[8,128]{1,0:T(8,128)S(1)}) custom-call(s32[8,64]{1,0:T(8,128)S(1)} %bitcast.7, s32[64]{0:T(128)S(1)} %copy-done.3, s32[1]{0:T(128)S(6)} %copy.14.node_ref, bf16[49,128,256]{2,1,0:T(8,128)(2,1)S(1)} %get-tuple-element.9.recv_ref, bf16[64,8,128,128]{3,2,1,0:T(8,128)(2,1)} %tile_hbm.1, ...), custom_call_target="tpu_custom_call" | custom-call | tf_op jit(solution)/shard_map/pallas_call | solution.py:354
  39.6 11.1 %shard_map.129.totals_ref = f32[8,128]{1,0:T(8,128)S(1)} custom-call(f32[8,128]{1,0:T(8,128)S(1)} %get-tuple-element.11.stats_ref), custom_call_target="tpu_custom_call" | custom-call | tf_op jit(solution)/shard_map/pallas_call | solution.py:413
  50.8 0.0 copy-done.1
  50.8 0.0 copy-done.4
  50.8 0.0 copy-done.5
  50.8 0.0 copy-done.6
  50.8 4.6 %shard_map.130 = bf16[8192,256]{1,0:T(8,128)(2,1)} custom-call(s32[1]{0:T(128)S(6)} %copy.14.node_ref, f32[8,128]{1,0:T(8,128)S(1)} %shard_map.129.totals_ref, bf16[8192,256]{1,0:T(8,128)(2,1)S(1)} %get-tuple-element.12.combined_ref, bf16[256,256]{1,0:T(8,128)(2,1)S(1)} %copy-done, f32[1,256]{1,0:T(1,128)S(1)} %bitcast.8, f32[1,256]{1,0:T(1,128)S(1)} %bitcast.9, ...), custom_call_target="tpu_custom_call" | custom-call | tf_op jit(solution)/shard_map/pallas_call | solution.py:501
Async XLA Ops:
  0.7 28.1 %copy-start = (bf16[256,256]{1,0:T(8,128)(2,1)S(1)}, bf16[256,256]{1,0:T(8,128)(2,1)}, u32[]{:S(2)}) copy-start(bf16[256,256]{1,0:T(8,128)(2,1)} %w1_ref.1) | copy-start | bytes 393220
  0.7 28.1 %copy-start.2 = (s32[64,8]{0,1:T(8,128)S(1)}, s32[64,8]{0,1:T(8,128)}, u32[]{:S(2)}) copy-start(s32[64,8]{0,1:T(8,128)} %param.17) | copy-start | bytes 6148
  0.7 28.1 %copy-start.3 = (s32[64]{0:T(128)S(1)}, s32[64]{0:T(128)}, u32[]{:S(2)}) copy-start(s32[64]{0:T(128)} %count_ref.1) | copy-start | bytes 772
  28.8 22.0 %copy-start.1 = (bf16[256,256]{1,0:T(8,128)(2,1)S(1)}, bf16[256,256]{1,0:T(8,128)(2,1)}, u32[]{:S(2)}) copy-start(bf16[256,256]{1,0:T(8,128)(2,1)} %w2_ref.1) | copy-start | bytes 393220
  28.8 22.0 %copy-start.4 = (f32[256]{0:T(256)S(1)}, f32[256]{0:T(256)}, u32[]{:S(2)}) copy-start(f32[256]{0:T(256)} %param.24) | copy-start | bytes 3076
  28.8 22.0 %copy-start.5 = (f32[256]{0:T(256)S(1)}, f32[256]{0:T(256)}, u32[]{:S(2)}) copy-start(f32[256]{0:T(256)} %param.25) | copy-start | bytes 3076
  28.8 22.0 %copy-start.6 = (f32[256]{0:T(256)S(1)}, f32[256]{0:T(256)}, u32[]{:S(2)}) copy-start(f32[256]{0:T(256)} %param.27) | copy-start | bytes 3076

commit v4 on v3

--- a/solution.py
+++ b/solution.py
@@ -13,7 +13,7 @@
 F32 = jnp.float32
 DEPTH = 4
 BATCH = 4
-REMOTE_LIMIT = 32
+REMOTE_LIMIT = 14
 FINISH_LIMIT = 16
 GROUP = 8
 
@@ -25,11 +25,15 @@
     return inner, outer
 
 
+def greet(partners):
+    for device, _ in partners:
+        pl.semaphore_signal(
+            pltpu.get_barrier_semaphore(), inc=1, device_id=device, device_id_type=MESH
+        )
+
+
 def enter(partners):
-    barrier = pltpu.get_barrier_semaphore()
-    for device, _ in partners:
-        pl.semaphore_signal(barrier, inc=1, device_id=device, device_id_type=MESH)
-    pl.semaphore_wait(barrier, len(partners))
+    pl.semaphore_wait(pltpu.get_barrier_semaphore(), len(partners))
 
 
 def exchange_kernel(
@@ -83,10 +87,11 @@
             )
         )
     ]
+    feats = pltpu.make_async_copy(feat_ref, table.at[pl.ds(0, nb)], feat_sem)
+    feats.start()
     for copy in lists:
         copy.start()
-    feats = pltpu.make_async_copy(feat_ref, table.at[pl.ds(0, nb)], feat_sem)
-    feats.start()
+    greet(inner + outer)
 
     def tile_copy(g, slot):
         return pltpu.make_async_copy(
@@ -244,30 +249,21 @@
     count_ref,
     node_ref,
     recv_ref,
-    tile_hbm,
+    tile_ref,
     part_ref,
     w_ref,
     out_ref,
     stats_ref,
-    tile_ref,
     total_ref,
     code_ref,
     found_ref,
     extra_ref,
-    tile_sem,
 ):
     nb, per_block, rows = tile_ref.shape[:3]
     width = part_ref.shape[2]
     zero_slot = recv_ref.shape[0] - 1
     filled = node_ref[0]
     steps = nb // GROUP
-
-    def tile_copy(step):
-        some = pl.ds(step * GROUP, GROUP)
-        return pltpu.make_async_copy(tile_hbm.at[some], tile_ref.at[some], tile_sem.at[step])
-
-    for step in range(steps):
-        tile_copy(step).start()
 
     def pair_product(b, code, n, pair):
         weights, sources = [], []
@@ -284,7 +280,6 @@
         )
 
     def first_pairs(step, extra):
-        tile_copy(step).wait()
         for g in range(GROUP):
             b = step * GROUP + g
             used = count_ref[b]
@@ -350,22 +345,19 @@
     lines = -(-(2 * (w_first.shape[1] // 128) + 1) // 8) * 8
     smem = pl.BlockSpec(memory_space=pltpu.SMEM)
     vmem = pl.BlockSpec(memory_space=pltpu.VMEM)
-    hbm = pl.BlockSpec(memory_space=pltpu.HBM)
     return pl.pallas_call(
         remote_kernel,
-        in_specs=[smem, smem, smem, vmem, hbm, vmem, vmem],
+        in_specs=[smem, smem, smem, vmem, vmem, vmem, vmem],
         out_specs=(vmem, vmem),
         out_shape=(
             jax.ShapeDtypeStruct((nb * rows, width), BF16),
             jax.ShapeDtypeStruct((lines, 128), F32),
         ),
         scratch_shapes=[
-            pltpu.VMEM(tiles.shape, BF16),
             pltpu.VMEM((nb, rows, width), F32),
             pltpu.SMEM((nb,), jnp.int32),
             pltpu.SMEM((nb,), jnp.int32),
             pltpu.SMEM((nb * per_block // 2 + BATCH,), jnp.int32),
-            pltpu.SemaphoreType.DMA((nb // GROUP,)),
         ],
         compiler_params=pltpu.CompilerParams(vmem_limit_bytes=REMOTE_LIMIT << 20),
     )(
@@ -373,7 +365,7 @@
         tile_count,
         node_count,
         recv,
-        pltpu.with_memory_space_constraint(tiles, pltpu.HBM),
+        tiles,
         part,
         w_first,
     )
@@ -382,6 +374,7 @@
 def totals_kernel(n_inner, n_outer, stats_ref, out_ref, first_buf, second_buf, mid, send_sem, recv_sem):
     i, o = lax.axis_index("inner"), lax.axis_index("outer")
     inner, outer = peers_of(n_inner, n_outer)
+    greet(inner + outer)
     enter(inner + outer)
 
     def round_of(partners, source, buf, me, base):

time: 55.9 us -> 54.5 us (0.975)
  Pallas kernels: 54.6 us -> 53 us
    pallas_call x1, Pallas kernels: 10.8 us -> 8.89 us  [remote_tiles(): pl.pallas_call(remote_kernel, in_specs=[smem, smem, smem, vmem, vmem, vme...]
where the time goes in v4:
time: 54.5 us; the launch traced here: 53.9 us
  Pallas kernels  53 us (97%)
  between operations  0.8 us (1%)
    pallas_call x1, Pallas kernels, exchange(): pl.pallas_call(functools.partial(exchange_kernel, n_inner, n_outer), out_...  28.1 us
    pallas_call x1, Pallas kernels, all_totals(): pl.pallas_call(functools.partial(totals_kernel, n_inner, n_outer), out_sh...  11.5 us
    pallas_call x1, Pallas kernels, remote_tiles(): pl.pallas_call(remote_kernel, in_specs=[smem, smem, smem, vmem, vmem, vme...  8.89 us
    pallas_call x1, Pallas kernels, finish(): pl.pallas_call(finish_kernel, in_specs=[smem] + [vmem] * 7, out_specs=pl....  4.61 us

profile of v4, /device:TPU:0, one launch (start us, length us, event | category | flops | bytes accessed | tf_op | source)
XLA Modules:
  0.0 53.9 jit_solution(11458222529957326935)
XLA Ops:
  0.7 0.0 copy-start
  0.7 0.0 copy-start.1
  0.7 0.0 copy-start.3
  0.7 0.0 copy-start.4
  0.7 28.1 %shard_map.127 = (bf16[49,128,256]{2,1,0:T(8,128)(2,1)S(1)}, f32[64,128,256]{2,1,0:T(8,128)S(1)}) custom-call(s32[1]{0:T(128)S(6)} %copy.14.node_ref, s32[8,64]{1,0:T(8,128)} %bitcast.6, s32[64]{0:T(128)} %count_ref.1, s32[1,8]{1,0:T(1,128)} %border_hbm.1, s32[1,4,4]{2,1,0:T(4,128)} %send_in_hbm.1, s32[1,4,8]{2,1,0:T(4,128)} %bitcast.12, ...), custom_call_target="tpu_custom_call" | custom-call | tf_op jit(solution)/shard_map/pallas_call | solution.py:208
  28.8 0.0 copy-done
  28.8 0.0 copy-done.1
  28.8 0.0 copy-done.3
  28.8 0.0 copy-done.4
  28.8 0.0 copy-start.2
  28.8 0.0 copy-start.5
  28.8 0.0 copy-start.6
  28.8 0.0 copy-start.7
  28.8 8.9 %shard_map.128 = (bf16[8192,256]{1,0:T(8,128)(2,1)S(1)}, f32[8,128]{1,0:T(8,128)S(1)}) custom-call(s32[8,64]{1,0:T(8,128)S(1)} %bitcast.7, s32[64]{0:T(128)S(1)} %copy-done.4, s32[1]{0:T(128)S(6)} %copy.14.node_ref, bf16[49,128,256]{2,1,0:T(8,128)(2,1)S(1)} %get-tuple-element.9.recv_ref, bf16[64,8,128,128]{3,2,1,0:T(8,128)(2,1)S(1)} %copy-done, ...), custom_call_target="tpu_custom_call" | custom-call | tf_op jit(solution)/shard_map/pallas_call | solution.py:348
  37.7 11.5 %shard_map.129.totals_ref = f32[8,128]{1,0:T(8,128)S(1)} custom-call(f32[8,128]{1,0:T(8,128)S(1)} %get-tuple-element.11.stats_ref), custom_call_target="tpu_custom_call" | custom-call | tf_op jit(solution)/shard_map/pallas_call | solution.py:406
  49.2 0.0 copy-done.2
  49.2 0.0 copy-done.5
  49.3 0.0 copy-done.6
  49.3 0.0 copy-done.7
  49.3 4.6 %shard_map.130 = bf16[8192,256]{1,0:T(8,128)(2,1)} custom-call(s32[1]{0:T(128)S(6)} %copy.14.node_ref, f32[8,128]{1,0:T(8,128)S(1)} %shard_map.129.totals_ref, bf16[8192,256]{1,0:T(8,128)(2,1)S(1)} %get-tuple-element.12.combined_ref, bf16[256,256]{1,0:T(8,128)(2,1)S(1)} %copy-done.1, f32[1,256]{1,0:T(1,128)S(1)} %bitcast.8, f32[1,256]{1,0:T(1,128)S(1)} %bitcast.9, ...), custom_call_target="tpu_custom_call" | custom-call | tf_op jit(solution)/shard_map/pallas_call | solution.py:494
Async XLA Ops:
  0.7 28.1 %copy-start = (bf16[64,8,128,128]{3,2,1,0:T(8,128)(2,1)S(1)}, bf16[64,8,128,128]{3,2,1,0:T(8,128)(2,1)}, u32[]{:S(2)}) copy-start(bf16[64,8,128,128]{3,2,1,0:T(8,128)(2,1)} %tile_ref.3) | copy-start | bytes 50331652
  0.7 28.1 %copy-start.1 = (bf16[256,256]{1,0:T(8,128)(2,1)S(1)}, bf16[256,256]{1,0:T(8,128)(2,1)}, u32[]{:S(2)}) copy-start(bf16[256,256]{1,0:T(8,128)(2,1)} %w1_ref.1) | copy-start | bytes 393220
  0.7 28.1 %copy-start.3 = (s32[64,8]{0,1:T(8,128)S(1)}, s32[64,8]{0,1:T(8,128)}, u32[]{:S(2)}) copy-start(s32[64,8]{0,1:T(8,128)} %param.17) | copy-start | bytes 6148
  0.7 28.1 %copy-start.4 = (s32[64]{0:T(128)S(1)}, s32[64]{0:T(128)}, u32[]{:S(2)}) copy-start(s32[64]{0:T(128)} %count_ref.1) | copy-start | bytes 772
  28.8 20.4 %copy-start.2 = (bf16[256,256]{1,0:T(8,128)(2,1)S(1)}, bf16[256,256]{1,0:T(8,128)(2,1)}, u32[]{:S(2)}) copy-start(bf16[256,256]{1,0:T(8,128)(2,1)} %w2_ref.1) | copy-start | bytes 393220
  28.8 20.4 %copy-start.5 = (f32[256]{0:T(256)S(1)}, f32[256]{0:T(256)}, u32[]{:S(2)}) copy-start(f32[256]{0:T(256)} %param.24) | copy-start | bytes 3076
  28.8 20.4 %copy-start.6 = (f32[256]{0:T(256)S(1)}, f32[256]{0:T(256)}, u32[]{:S(2)}) copy-start(f32[256]{0:T(256)} %param.25) | copy-start | bytes 3076
  28.8 20.4 %copy-start.7 = (f32[256]{0:T(256)S(1)}, f32[256]{0:T(256)}, u32[]{:S(2)}) copy-start(f32[256]{0:T(256)} %param.27) | copy-start | bytes 3076
